TPU v7x, 32 devices: a whole 2x2x4 slice. The times are simulated.
32 devices in a mesh: dom: 8 (over z, x), rep: 4 (over y, core).
Axes of the slice: x: 2, y: 2, z: 4, core: 2. Of those that a mesh axis runs over, the one named last changes fastest.
Arguments:
- spline_blocks: bfloat16 [256, 2, 64, 128], P(('dom', 'rep')), may hold values from -0.75 to 0.75
- modal_coeff: bfloat16 [64, 2, 8], replicated, may hold values from -6 to 6
- frequency: float32 [8], replicated, may hold values from 0.2 to 0.8
- face_dest: int32 [32768, 1], P('dom'), may hold values from 0 to 7; in each aligned block of 4096 rows (0 to 4095, 4096 to 8191, ...) at most 1024 rows name the same one
- face_cell: int32 [32768], P('dom'), may hold values from 0 to 2047
- wall_weight: float32 [5, 2, 16384], P(None, None, 'dom'), may hold values from -6 to 6
- flow_rhs: float32 [5, 2, 8, 16384], P(None, None, 'rep', 'dom'), may hold values from -6 to 6
- previous: float32 [5, 2, 8, 16384], P(None, None, 'rep', 'dom'), may hold values from -6 to 6
- diag_inverse: float32 [5, 5, 16384], P(None, None, 'dom'), may hold values from -0.3 to 1.2
- off_jacobian: bfloat16 [6, 5, 5, 16384], P(None, None, None, 'dom'), may hold values from -0.5 to 0.5
- neighbor: int32 [6, 16384], P(None, 'dom'), may hold values from 0 to 3071, as said below
- send_list: int32 [4, 2048], P(None, 'dom'), may hold values from 0 to 2047
Outputs:
- solution: float32 [5, 2, 8, 16384], P(None, None, 'rep', 'dom')
Inputs may be any that keep to these rules, and one draw needn't show every extreme that they name: `face_dest`: in each aligned block of 4096 rows (the rows of one index of dom), no partition is named by more than 1024 rows, and in every draw some partition is named by exactly 1024 rows of some block. `neighbor`: entries below 2048 name a cell of the same partition; entry 2048 + k * 256 + i names ghost row i of block k.
All inputs are finite; a program needn't handle non-finite values.
Results may differ from a plain program's by a relative error of at most 0.0003.
Values may be sent and summed in bfloat16 or wider, within the bound.
A program may use at most 64 MiB of HBM per device.

v0:
```python
import jax
import jax.numpy as jnp
from jax import lax
from jax.sharding import PartitionSpec as P

SWEEPS = 2


def from_behind(value, axis, by):
    length = lax.axis_size(axis)
    return lax.ppermute(value, axis, [(i, (i + by) % length) for i in range(length)])


def face_values(blocks_in, coeff_in, freq_in):
    mode_count = coeff_in.shape[0]
    column_count = coeff_in.shape[2]
    flat_coeff = coeff_in.reshape(mode_count, 2 * column_count)
    products = jnp.einsum(
        "kqmr,mz->qzkr", blocks_in, flat_coeff, preferred_element_type=jnp.float32
    )
    products = products.reshape(2, 2, column_count, blocks_in.shape[0] * blocks_in.shape[3])
    angular = freq_in[:, None]
    velocity = jnp.stack([-angular * products[0, 1], angular * products[0, 0]])
    return jnp.stack([velocity, products[1]])


def shards(
    spline_blocks,
    modal_coeff,
    frequency,
    face_dest,
    face_cell,
    wall_weight,
    flow_rhs,
    previous,
    diag_inverse,
    off_jacobian,
    neighbor,
    send_list,
):
    pair_dev = flow_rhs.shape[2]
    cell_count = flow_rhs.shape[3]
    dom_size = lax.axis_size("dom")
    first_pair = lax.axis_index("rep") * pair_dev
    own_freq = lax.dynamic_slice_in_dim(frequency, first_pair, pair_dev, 0)
    own_coeff = lax.dynamic_slice_in_dim(modal_coeff, first_pair, pair_dev, 2)
    face_data = face_values(
        lax.all_gather(spline_blocks, "rep", axis=0, tiled=True), own_coeff, own_freq
    )
    row_count = face_data.shape[3]
    capacity = 2 * row_count // dom_size
    destination = face_dest[:, 0]
    one_hot = (destination[:, None] == jnp.arange(dom_size, dtype=jnp.int32)[None, :]).astype(
        jnp.int32
    )
    position = jnp.sum(jnp.cumsum(one_hot, axis=0) * one_hot, axis=1) - 1
    slot_flat = destination * capacity + position
    values = face_data.reshape(4 * pair_dev, row_count)
    send_values = (
        jnp.zeros((4 * pair_dev, dom_size * capacity), jnp.float32).at[:, slot_flat].set(values)
    )
    send_cells = (
        jnp.full((1, dom_size * capacity), cell_count, jnp.float32)
        .at[0, slot_flat]
        .set(face_cell.astype(jnp.float32))
    )
    recv_values, recv_cells = (
        lax.all_to_all(
            send_values.reshape(4 * pair_dev, dom_size, capacity),
            "dom",
            split_axis=1,
            concat_axis=1,
            tiled=True,
        ),
        lax.all_to_all(
            send_cells.reshape(1, dom_size, capacity),
            "dom",
            split_axis=1,
            concat_axis=1,
            tiled=True,
        ),
    )
    cell_target = recv_cells.reshape(-1).astype(jnp.int32)
    wall_sum = (
        jnp.zeros((4 * pair_dev, cell_count), jnp.float32)
        .at[:, cell_target]
        .add(recv_values.reshape(4 * pair_dev, -1), mode="drop")
    )
    wall_sum = wall_sum.reshape(2, 2 * pair_dev, cell_count)
    row_width = 2 * pair_dev
    rhs_full = (
        flow_rhs.reshape(5, row_width, cell_count)
        + wall_weight[:, 0, None, :] * wall_sum[0][None]
        + wall_weight[:, 1, None, :] * wall_sum[1][None]
    )
    halo_count = send_list.shape[1]
    jac_faces = jnp.transpose(off_jacobian, (1, 2, 0, 3))
    neighbor_flat = neighbor.reshape(-1)
    angular = own_freq[None, :, None]
    iterate = previous
    for sweep_index in range(SWEEPS):
        flat_field = iterate.reshape(5 * row_width, cell_count)
        picked = jnp.take(flat_field, send_list.reshape(-1), axis=1)
        from_below = from_behind(picked[:, 0:halo_count], "dom", 1)
        from_above = from_behind(picked[:, halo_count : 2 * halo_count], "dom", -1)
        far_below = from_behind(picked[:, 2 * halo_count : 3 * halo_count], "dom", 2)
        far_above = from_behind(picked[:, 3 * halo_count :], "dom", -2)
        extended = jnp.concatenate(
            [flat_field, from_below, from_above, far_below, far_above], axis=1
        )
        beside = jnp.take(extended, neighbor_flat, axis=1).reshape(5, row_width, 6, cell_count)
        coupling = jnp.sum(
            jac_faces[:, :, None, :, :].astype(jnp.float32) * beside[None], axis=(1, 3)
        )
        spinning = jnp.stack([-angular * iterate[:, 1], angular * iterate[:, 0]], axis=1).reshape(
            5, row_width, cell_count
        )
        residual_now = rhs_full - coupling - spinning
        update = jnp.sum(diag_inverse[:, :, None, :] * residual_now[None], axis=1)
        iterate = update.reshape(5, 2, pair_dev, cell_count)
    return iterate


def solution(mesh):
    return jax.shard_map(
        shards,
        mesh=mesh,
        in_specs=(
            P(("dom", "rep"), None, None, None),
            P(),
            P(),
            P("dom", None),
            P("dom"),
            P(None, None, "dom"),
            P(None, None, "rep", "dom"),
            P(None, None, "rep", "dom"),
            P(None, None, "dom"),
            P(None, None, None, "dom"),
            P(None, "dom"),
            P(None, "dom"),
        ),
        out_specs=P(None, None, "rep", "dom"),
        check_vma=False,
    )
```

profile of v0, /device:TPU:0, one launch (start us, length us, event | category | flops | bytes accessed | tf_op | source)
XLA Modules:
  0.0 306.0 jit_solution(2823805454818781097)
XLA Ops:
  6.5 0.7 copy.103
  7.3 1.0 reshape.205
  8.3 0.4 copy.92
  8.7 2.8 gather_fusion
  11.5 0.2 select_bitcast_fusion.3
  11.8 0.8 fusion.17
  12.6 2.9 collective-permute-start
  15.5 3.0 collective-permute-start.1
  18.6 3.8 %collective-permute-start.3 = (f32[20,256]{0,1:T(8,128)}, f32[20,256]{0,1:T(8,128)}, u32[]{:S(2)}, u32[]{:S(2)}) collective-permute-start(f32[20,256]{0,1:T(8,128)} %get-tuple-element.15), channel_id=1, source_target_pairs={{0,24},{4,28},{8,0},{12,4},{16,8},{20,12},{24,16},{28,20},{1,25},{... | collective-permute-start | bytes 61448 | tf_op jit(solution)/shard_map/ppermute | solution.py:11
  22.4 2.3 reduce-window.6
  24.7 0.3 slice_reduce_fusion
  25.8 16.1 %scatter_custom_fusion.2 = f32[8192]{0:T(1024)} fusion(s32[4096]{0:T(1024)S(1)} %broadcast_select_fusion, f32[4096]{0:T(1024)S(1)} %convert_element_type.30, f32[]{:T(128)} %constant.9.clone.1), kind=kCustom, calls=%fused_computation.64 | custom fusion | bytes 32772
  41.9 4.0 %all-to-all-start = ((f32[1,8,1024]{2,0,1:T(1,128)}), f32[1,8,1024]{2,0,1:T(1,128)}, u32[]{:S(2)}, u32[]{:S(2)}) async-start(f32[1,8,1024]{2,0,1:T(1,128)} %bitcast.5), calls=%async_computation | async-start | bytes 65536 | tf_op jit(solution)/shard_map/all_to_all | solution.py:75
  45.9 0.7 all-gather.2.cloned.1.call-update
  46.7 0.6 fusion.7
  47.4 1.3 convert_bitcast_fusion
  48.8 0.7 fusion.14
  49.7 0.7 copy_bitcast_fusion
  50.4 0.5 constant_dynamic-slice_fusion
  51.1 1.1 reshape.197
  52.2 0.9 constant_dynamic-update-slice_fusion.3
  53.1 0.9 constant_dynamic-update-slice_fusion.2
  54.0 0.9 constant_dynamic-update-slice_fusion.1
  55.0 0.9 constant_dynamic-update-slice_fusion
  55.9 45.3 %gather_fusion.1 = f32[12288,20]{1,0:T(8,128)} fusion(f32[20,3072]{0,1:T(8,128)S(1)} %constant_dynamic-update-slice_fusion, s32[12288]{0:T(1024)} %fusion.7), kind=kCustom, calls=%fused_computation.1.clone | custom fusion | bytes 2015232 | tf_op jit(solution)/shard_map/jit(_take)/gather | solution.py:111
  101.2 10.3 %select_bitcast_fusion.1 = f32[20,12288]{0,1:T(8,128)} fusion(f32[12288,20]{1,0:T(8,128)} %gather_fusion.1, pred[12288]{0:T(1024)(128)(4,1)S(1)} %compare_and_fusion), kind=kLoop, calls=%fused_computation.8 | loop fusion | flops 245760 | bytes 1978368 | tf_op jit(solution)/shard_map/jit(_take)/select_n | solution.py:111
  111.5 5.5 %copy.93 = f32[20,12288]{1,0:T(8,128)} copy(f32[20,12288]{0,1:T(8,128)} %select_bitcast_fusion.1) | data formatting | bytes 1966080 | tf_op jit(solution)/shard_map/jit(_take)/select_n | solution.py:111
  117.0 1.8 mul.189
  118.8 0.6 copy.94
  119.4 1.7 multiply_reduce_fusion.1
  121.2 0.8 convert_element_type.31
  122.0 1.5 convolution_bitcast_fusion
  124.0 1.9 copy.85
  125.9 13.1 %scatter_custom_fusion = f32[8,8192]{0,1:T(8,128)} fusion(s32[4096]{0:T(1024)} %bitcast.71, f32[4096,8]{1,0:T(8,128)} %copy.85, f32[]{:T(128)} %constant.8.clone.1), kind=kCustom, calls=%fused_computation.11 | custom fusion | bytes 262656 | tf_op jit(solution)/shard_map/scatter | solution.py:60
  139.0 3.5 %copy.86 = f32[8,8,1024]{2,0,1:T(8,128)} copy(f32[8,8,1024]{0,2,1:T(8,128)} %bitcast.65) | data formatting | bytes 524288 | tf_op jit(solution)/shard_map/reshape | solution.py:69
  142.5 5.9 %all-to-all-start.1 = ((f32[8,8,1024]{2,0,1:T(8,128)}), f32[8,8,1024]{2,0,1:T(8,128)S(1)}, u32[]{:S(2)}, u32[]{:S(2)}) async-start(f32[8,8,1024]{2,0,1:T(8,128)} %copy.86), calls=%async_computation.1 | async-start | bytes 524288 | tf_op jit(solution)/shard_map/all_to_all | solution.py:68
  148.4 8.2 %all-to-all-done.1 = f32[8,8,1024]{2,0,1:T(8,128)S(1)} async-done(((f32[8,8,1024]{2,0,1:T(8,128)}), f32[8,8,1024]{2,0,1:T(8,128)S(1)}, u32[]{:S(2)}, u32[]{:S(2)}) %all-to-all-start.1) | async-done | bytes 262176 | tf_op jit(solution)/shard_map/all_to_all | solution.py:68
  156.6 2.6 copy.87
  159.2 44.6 %scatter_custom_fusion.1 = f32[8,2048]{0,1:T(8,128)S(1)} fusion(s32[8192]{0:T(1024)S(1)} %bitcast.76, f32[8192,8]{1,0:T(8,128)} %copy.87, f32[]{:T(128)} %constant.8.clone.1), kind=kCustom, calls=%fused_computation.19 | custom fusion | flops 65536 | bytes 66048 | tf_op jit(solution)/shard_map/scatter-add | solution.py:87
  203.7 1.7 fusion.15
  205.4 1.7 copy.90
  207.1 1.0 copy.88
  208.0 1.1 subtract_subtract_fusion.1
  209.1 0.2 multiply_reduce_fusion.3
  209.5 1.3 copy.96
  210.9 1.3 constant_dynamic-update-slice_fusion.9
  212.2 5.6 %gather_fusion.2 = f32[1024,20]{1,0:T(8,128)} fusion(f32[20,2048]{0,1:T(8,128)} %copy.96, s32[1024]{0:T(1024)} %copy-done.15), kind=kCustom, calls=%fused_computation.2.clone | custom fusion | bytes 167936 | tf_op jit(solution)/shard_map/jit(_take)/gather | solution.py:103
  217.8 0.8 slice_multiply_fusion.1
  218.6 1.2 select_bitcast_fusion.2
  219.8 0.8 fusion.16
  220.6 1.2 collective-permute-start.4
  221.9 0.8 reshape.210
  222.7 3.5 %collective-permute-start.5 = (f32[20,256]{0,1:T(8,128)}, f32[20,256]{0,1:T(8,128)S(1)}, u32[]{:S(2)}, u32[]{:S(2)}) collective-permute-start(f32[20,256]{0,1:T(8,128)} %get-tuple-element.13), channel_id=1, source_target_pairs={{0,28},{4,0},{8,4},{12,8},{16,12},{20,16},{24,20},{28,24},{1,29},{... | collective-permute-start | bytes 61448 | tf_op jit(solution)/shard_map/ppermute | solution.py:11
  226.3 3.8 %collective-permute-start.7 = (f32[20,256]{0,1:T(8,128)}, f32[20,256]{0,1:T(8,128)S(1)}, u32[]{:S(2)}, u32[]{:S(2)}) collective-permute-start(f32[20,256]{0,1:T(8,128)} %get-tuple-element.11), channel_id=1, source_target_pairs={{0,24},{4,28},{8,0},{12,4},{16,8},{20,12},{24,16},{28,20},{1,25},{... | collective-permute-start | bytes 61448 | tf_op jit(solution)/shard_map/ppermute | solution.py:11
  230.1 0.9 constant_dynamic-update-slice_fusion.8
  231.0 2.2 collective-permute-done.6
  233.3 45.3 %gather_fusion.3 = f32[12288,20]{1,0:T(8,128)} fusion(f32[20,3072]{0,1:T(8,128)S(1)} %constant_dynamic-update-slice_fusion.5, s32[12288]{0:T(1024)} %fusion.7), kind=kCustom, calls=%fused_computation.3.clone | custom fusion | bytes 2015232 | tf_op jit(solution)/shard_map/jit(_take)/gather | solution.py:111
  278.6 10.3 %select_bitcast_fusion = f32[20,12288]{0,1:T(8,128)} fusion(f32[12288,20]{1,0:T(8,128)} %gather_fusion.3, pred[12288]{0:T(1024)(128)(4,1)S(1)} %compare_and_fusion), kind=kLoop, calls=%fused_computation.7 | loop fusion | flops 245760 | bytes 1978368 | tf_op jit(solution)/shard_map/jit(_take)/select_n | solution.py:111
  288.9 5.5 %copy.97 = f32[20,12288]{1,0:T(8,128)} copy(f32[20,12288]{0,1:T(8,128)} %select_bitcast_fusion) | data formatting | bytes 1966080 | tf_op jit(solution)/shard_map/jit(_take)/select_n | solution.py:111
  294.4 1.8 mul.198
  296.2 0.6 copy.98
  296.9 1.1 multiply_reduce_fusion
  298.1 0.2 multiply_reduce_fusion.2
  298.3 0.8 reshape.211
  (98 shorter events, 2.3 us)
Async XLA Ops:
  6.5 43.9 %copy-start = (bf16[64,2,8]{0,2,1:T(8,128)(2,1)S(1)}, bf16[64,2,8]{0,2,1:T(8,128)(2,1)}, u32[]{:S(2)}) copy-start(bf16[64,2,8]{0,2,1:T(8,128)(2,1)} %param.17) | copy-start | bytes 6148
  7.2 4.5 %copy-start.15 = (s32[1024]{0:T(1024)}, s32[1024]{0:T(1024)S(1)}, u32[]{:S(2)}) copy-start(s32[1024]{0:T(1024)S(1)} %fusion.13) | copy-start | bytes 12292
  7.3 4.5 %copy-start.17 = (pred[1024]{0:T(1024)(128)(4,1)}, pred[1024]{0:T(1024)(128)(4,1)S(1)}, u32[]{:S(2)}) copy-start(pred[1024]{0:T(1024)(128)(4,1)S(1)} %compare_and_fusion.1) | copy-start | bytes 3076
  8.7 13.7 %copy-start.11 = (s32[4096,1]{0,1:T(1,128)S(1)}, s32[4096,1]{0,1:T(1,128)}, u32[]{:S(2)}) copy-start(s32[4096,1]{0,1:T(1,128)} %param.19) | copy-start | bytes 49156
  11.5 14.0 %copy-start.24 = (s32[2]{0:T(128)S(1)}, s32[2]{0:T(128)}, u32[]{:S(2)}) copy-start(s32[2]{0:T(128)} %constant.60) | copy-start | bytes 28
  11.5 14.1 %copy-start.23 = (s32[2]{0:T(128)S(1)}, s32[2]{0:T(128)}, u32[]{:S(2)}) copy-start(s32[2]{0:T(128)} %constant.21) | copy-start | bytes 28
  11.5 14.2 %copy-start.16 = (s32[4096]{0:T(1024)S(1)}, s32[4096]{0:T(1024)}, u32[]{:S(2)}) copy-start(s32[4096]{0:T(1024)} %param.20) | copy-start | bytes 49156
  12.6 39.6 %collective-permute-start = (f32[20,256]{0,1:T(8,128)}, f32[20,256]{0,1:T(8,128)}, u32[]{:S(2)}, u32[]{:S(2)}) collective-permute-start(f32[20,256]{0,1:T(8,128)} %get-tuple-element.18), channel_id=1, source_target_pairs={{0,4},{4,8},{8,12},{12,16},{16,20},{20,24},{24,28},{28,0},{1,5},{5... | collective-permute-start | bytes 61448 | tf_op jit(solution)/shard_map/ppermute | solution.py:11
  15.5 37.6 %collective-permute-start.1 = (f32[20,256]{0,1:T(8,128)}, f32[20,256]{0,1:T(8,128)}, u32[]{:S(2)}, u32[]{:S(2)}) collective-permute-start(f32[20,256]{0,1:T(8,128)} %get-tuple-element.17), channel_id=1, source_target_pairs={{0,28},{4,0},{8,4},{12,8},{16,12},{20,16},{24,20},{28,24},{1,29},{... | collective-permute-start | bytes 61448 | tf_op jit(solution)/shard_map/ppermute | solution.py:11
  18.6 35.5 %collective-permute-start.2 = (f32[20,256]{0,1:T(8,128)}, f32[20,256]{0,1:T(8,128)}, u32[]{:S(2)}, u32[]{:S(2)}) collective-permute-start(f32[20,256]{0,1:T(8,128)} %get-tuple-element.16), channel_id=1, source_target_pairs={{0,8},{4,12},{8,16},{12,20},{16,24},{20,28},{24,0},{28,4},{1,9},{5... | collective-permute-start | bytes 61448 | tf_op jit(solution)/shard_map/ppermute | solution.py:11
  18.6 36.4 %collective-permute-start.3 = (f32[20,256]{0,1:T(8,128)}, f32[20,256]{0,1:T(8,128)}, u32[]{:S(2)}, u32[]{:S(2)}) collective-permute-start(f32[20,256]{0,1:T(8,128)} %get-tuple-element.15), channel_id=1, source_target_pairs={{0,24},{4,28},{8,0},{12,4},{16,8},{20,12},{24,16},{28,20},{1,25},{... | collective-permute-start | bytes 61448 | tf_op jit(solution)/shard_map/ppermute | solution.py:11
  25.0 21.7 %copy-start.14 = (s32[6,2048]{1,0:T(8,128)S(1)}, s32[6,2048]{1,0:T(8,128)}, u32[]{:S(2)}) copy-start(s32[6,2048]{1,0:T(8,128)} %param.26) | copy-start | bytes 147460
  25.5 21.9 %copy-start.12 = (s32[4096,1]{0,1:T(1,128)}, s32[4096,1]{0,1:T(1,128)S(1)}, u32[]{:S(2)}) copy-start(s32[4096,1]{0,1:T(1,128)S(1)} %compare_select_fusion.2) | copy-start | bytes 49156
  41.9 79.3 %all-to-all-start = ((f32[1,8,1024]{2,0,1:T(1,128)}), f32[1,8,1024]{2,0,1:T(1,128)}, u32[]{:S(2)}, u32[]{:S(2)}) async-start(f32[1,8,1024]{2,0,1:T(1,128)} %bitcast.5), calls=%async_computation | async-start | bytes 65536 | tf_op jit(solution)/shard_map/all_to_all | solution.py:75
  45.9 76.1 %all-gather.2.cloned.1.call-start = ((), (), s32[]{:S(2)}) async-start(), calls=%async_computation.2 | async-start | bytes 1310720 | tf_op jit(solution)/shard_map/all_gather | solution.py:48
  46.7 2.0 copy-start.13
  46.7 2.8 copy-start.4
  49.5 0.9 copy-start.18
  49.5 0.9 copy-start.20
  119.4 2.6 copy-start.22
  121.2 2.5 copy-start.19
  121.2 2.5 copy-start.21
  142.5 14.1 %all-to-all-start.1 = ((f32[8,8,1024]{2,0,1:T(8,128)}), f32[8,8,1024]{2,0,1:T(8,128)S(1)}, u32[]{:S(2)}, u32[]{:S(2)}) async-start(f32[8,8,1024]{2,0,1:T(8,128)} %copy.86), calls=%async_computation.1 | async-start | bytes 524288 | tf_op jit(solution)/shard_map/all_to_all | solution.py:68
  205.4 1.7 copy-start.1
  205.4 3.7 %copy-start.2 = (f32[5,5,2048]{2,1,0:T(8,128)S(1)}, f32[5,5,2048]{2,1,0:T(8,128)}, u32[]{:S(2)}) copy-start(f32[5,5,2048]{2,1,0:T(8,128)} %param.24) | copy-start | bytes 614404
  207.1 2.5 copy-start.8
  220.6 9.4 %collective-permute-start.4 = (f32[20,256]{0,1:T(8,128)}, f32[20,256]{0,1:T(8,128)}, u32[]{:S(2)}, u32[]{:S(2)}) collective-permute-start(f32[20,256]{0,1:T(8,128)} %get-tuple-element.14), channel_id=1, source_target_pairs={{0,4},{4,8},{8,12},{12,16},{16,20},{20,24},{24,28},{28,0},{1,5},{5... | collective-permute-start | bytes 61448 | tf_op jit(solution)/shard_map/ppermute | solution.py:11
  222.7 8.3 %collective-permute-start.5 = (f32[20,256]{0,1:T(8,128)}, f32[20,256]{0,1:T(8,128)S(1)}, u32[]{:S(2)}, u32[]{:S(2)}) collective-permute-start(f32[20,256]{0,1:T(8,128)} %get-tuple-element.13), channel_id=1, source_target_pairs={{0,28},{4,0},{8,4},{12,8},{16,12},{20,16},{24,20},{28,24},{1,29},{... | collective-permute-start | bytes 61448 | tf_op jit(solution)/shard_map/ppermute | solution.py:11
  226.2 7.0 %collective-permute-start.6 = (f32[20,256]{0,1:T(8,128)}, f32[20,256]{0,1:T(8,128)S(1)}, u32[]{:S(2)}, u32[]{:S(2)}) collective-permute-start(f32[20,256]{0,1:T(8,128)} %get-tuple-element.12), channel_id=1, source_target_pairs={{0,8},{4,12},{8,16},{12,20},{16,24},{20,28},{24,0},{28,4},{1,9},{5... | collective-permute-start | bytes 61448 | tf_op jit(solution)/shard_map/ppermute | solution.py:11
  226.3 7.0 %collective-permute-start.7 = (f32[20,256]{0,1:T(8,128)}, f32[20,256]{0,1:T(8,128)S(1)}, u32[]{:S(2)}, u32[]{:S(2)}) collective-permute-start(f32[20,256]{0,1:T(8,128)} %get-tuple-element.11), channel_id=1, source_target_pairs={{0,24},{4,28},{8,0},{12,4},{16,8},{20,12},{24,16},{28,20},{1,25},{... | collective-permute-start | bytes 61448 | tf_op jit(solution)/shard_map/ppermute | solution.py:11
  296.8 1.1 copy-start.5
  296.8 1.1 copy-start.6
  296.8 1.1 copy-start.7
  296.9 1.1 copy-start.9
  296.9 1.1 copy-start.10
  296.9 1.2 copy-start.3
Sparse Core Ops, SparseCore 0:
  48.3 18.2 all-gather.1
where the time goes:
time: 309 us; the launch traced here: 306 us
  local copies, waits for them, and re-layouts  172 us (56%)
  other arithmetic  78.8 us (26%)
  starting transfers between devices  28.2 us (9%)
  between operations  14.1 us (5%)
  waiting for transfers between devices  11.1 us (4%)
    gather x2, local copies, waits for them, and re-layouts, shards(): jnp.take(extended, neighbor_flat, axis=1)  90.6 us
    scatter-add x1, other arithmetic, shards(): wall_sum = jnp.zeros((4 * pair_dev, cell_count), jnp.float32).at[:, cell_...  44.6 us
    unnamed x60, local copies, waits for them, and re-layouts  22 us
    select_n x2, other arithmetic, shards(): jnp.take(extended, neighbor_flat, axis=1)  20.7 us
    ppermute x8, starting transfers between devices, from_behind(): lax.ppermute(value, axis, [(i, (i + by) % length) for i in range(length)])  18.4 us
    scatter x1, local copies, waits for them, and re-layouts, shards(): jnp.zeros((4 * pair_dev, dom_size * capacity), jnp.float32).at[:, slot_flat]  13.1 us
    select_n x2, local copies, waits for them, and re-layouts, shards(): jnp.take(extended, neighbor_flat, axis=1)  11 us
    gather x2, local copies, waits for them, and re-layouts, shards(): picked = jnp.take(flat_field, send_list.reshape(-1), axis=1)  8.38 us
  transfers between devices with their start and end apart: 11, of which 2 were waited for; matrix products, arithmetic and copies ran while one was open for 32% of the time, Pallas kernels for 0%

commit v1 on v0

v1 whole, which is shorter than its diff:
```python
import functools

import jax
import jax.numpy as jnp
from jax import lax
from jax.experimental import pallas as pl
from jax.experimental.pallas import tpu as pltpu
from jax.sharding import PartitionSpec as P

SWEEPS = 2
OFFSETS = (1, -1, 2, -2)
LANES = 128
MESH = pl.DeviceIdType.MESH
F32 = jnp.float32
BF16 = jnp.bfloat16


def iota(shape, axis):
    return lax.broadcasted_iota(jnp.int32, shape, axis)


def split(value):
    high = value.astype(BF16)
    return high, (value - high.astype(F32)).astype(BF16)


def dot_last(a, b):
    return lax.dot_general(a, b, (((1,), (1,)), ((), ())), preferred_element_type=F32)


def lane_pick(table, index):
    return jnp.take_along_axis(table, index, axis=1, mode="promise_in_bounds")


class Plan:
    def __init__(self, dom, rep, spline, face_dest, flow_rhs, send_list):
        self.dom, self.rep = dom, rep
        self.blocks = spline.shape[0]
        self.faces = face_dest.shape[0]
        self.own_faces = self.faces // rep
        self.pairs = flow_rhs.shape[2]
        self.comps = flow_rhs.shape[0]
        self.cells = flow_rhs.shape[3]
        self.halo = send_list.shape[1]
        self.part_rows = 2 * self.pairs
        self.rows = self.comps * self.part_rows
        self.row_pad = -(-self.rows // 8) * 8
        self.values = 2 * self.part_rows
        self.cap = 2 * self.faces // dom
        self.width = min(2 * LANES, self.cap)
        self.steps = self.cap // self.width
        count = self.values + 1
        while count * self.steps % 8:
            count += 1
        self.slot_rows = count * self.steps
        self.chunks = self.cells // LANES
        self.halo_chunks = self.halo // LANES
        self.face_chunks = self.faces // LANES


def kernel(
    pn,
    freq_ref,
    spline_ref,
    coeff_ref,
    dest_ref,
    cell_ref,
    weight_ref,
    flow_ref,
    prev_ref,
    diag_ref,
    jac_ref,
    neighbor_ref,
    send_ref,
    out_ref,
    part_buf,
    face_buf,
    slot_buf,
    left_buf,
    right_buf,
    pack_buf,
    recv_buf,
    add_left,
    add_right,
    wall_buf,
    field,
    ghost,
    halo_send,
    beside,
    jac,
    diag,
    weight,
    flow,
    iterate,
    coupled,
    rep_send_sem,
    rep_recv_sem,
    dom_send_sem,
    dom_recv_sem,
    halo_send_sem,
    halo_recv_sem,
):
    me_dom, me_rep = lax.axis_index("dom"), lax.axis_index("rep")
    n_ch, rows, rpad, width = pn.chunks, pn.rows, pn.row_pad, pn.part_rows
    groups = rpad // 8

    barrier = pltpu.get_barrier_semaphore()
    for offset in range(1, pn.rep):
        pl.semaphore_signal(
            barrier, inc=1, device_id=(me_dom, lax.rem(me_rep + offset, pn.rep)), device_id_type=MESH
        )

    def greet(offset, carry):
        pl.semaphore_signal(
            barrier, inc=1, device_id=(lax.rem(me_dom + offset, pn.dom), me_rep), device_id_type=MESH
        )
        return carry

    lax.fori_loop(1, pn.dom, greet, 0)

    row_id = iota((pn.rep * pn.values, LANES), 0)
    pair_id = row_id // pn.values * pn.pairs + row_id % pn.pairs
    scale = jnp.zeros(row_id.shape, F32)
    for pair in range(pn.rep * pn.pairs):
        scale = jnp.where(pair_id == pair, freq_ref[pair], scale)
    scale = jnp.where(row_id // pn.pairs % 2 == 0, -scale, scale)
    scale = jnp.where(row_id // width % 2 == 0, scale, 1.0)
    for block in range(pn.blocks):
        base = jnp.dot(coeff_ref[...], spline_ref[block], preferred_element_type=F32) * scale
        for peer in range(pn.rep):
            part_buf[peer, :, block * LANES : (block + 1) * LANES] = base[
                peer * pn.values : (peer + 1) * pn.values
            ]

    pl.semaphore_wait(barrier, pn.rep - 1 + pn.dom - 1)

    def rep_copy(offset):
        peer = lax.rem(me_rep + offset, pn.rep)
        return pltpu.make_async_remote_copy(
            src_ref=part_buf.at[peer],
            dst_ref=face_buf.at[me_rep],
            send_sem=rep_send_sem.at[offset],
            recv_sem=rep_recv_sem.at[offset],
            device_id=(me_dom, peer),
            device_id_type=MESH,
        )

    for offset in range(1, pn.rep):
        rep_copy(offset).start()
    face_buf[me_rep] = part_buf[me_rep]

    group = min(8, pn.dom)
    lines = pn.face_chunks
    tri = jnp.where(
        (iota((LANES, 2 * LANES), 1) >= LANES)
        | (iota((LANES, 2 * LANES), 0) <= iota((LANES, 2 * LANES), 1)),
        1.0,
        0.0,
    ).astype(BF16)
    size = group * lines
    above = jnp.where(
        (iota((size, size), 0) // lines == iota((size, size), 1) // lines)
        & (iota((size, size), 1) < iota((size, size), 0)),
        1.0,
        0.0,
    ).astype(BF16)
    dest = dest_ref[...]
    slots = jnp.zeros((lines, LANES), F32)
    for first in range(0, pn.dom, group):
        mask = jnp.concatenate(
            [jnp.where(dest == first + d, 1.0, 0.0) for d in range(group)], axis=0
        )
        counts = jnp.dot(mask.astype(BF16), tri, preferred_element_type=F32)
        before = jnp.dot(above, counts[:, LANES:].astype(BF16), preferred_element_type=F32)
        place = mask * (counts[:, :LANES] + before - 1.0)
        for d in range(group):
            part = slice(d * lines, (d + 1) * lines)
            slots = slots + place[part] + mask[part] * float((first + d) * pn.cap)
    slot_buf[...] = slots.astype(jnp.int32)

    def unfold(source, target, base):
        for tile in range(n_ch):
            target[pl.ds(base + tile, source.shape[0], stride=n_ch), :] = source[
                :, tile * LANES : (tile + 1) * LANES
            ]

    def spread_field():
        for row in range(rows):
            field[pl.ds(row, n_ch, stride=rpad), :] = iterate[row * n_ch : (row + 1) * n_ch]

    def pick(table, first_chunk, count, index, start):
        low, high = index % LANES, index // LANES
        picked = list(start)
        for chunk in range(count):
            here = high == first_chunk + chunk
            for g in range(groups):
                found = lane_pick(table[pl.ds(chunk * rpad + g * 8, 8), :], low)
                picked[g] = jnp.where(here, found, picked[g])
        return picked

    def wide_row(ref, row, tile):
        line = ref[row : row + 1, pl.ds(pl.multiple_of(tile * LANES, LANES), LANES)]
        return jnp.broadcast_to(line, (8, LANES))

    zeros = [jnp.zeros((8, LANES), F32)] * groups

    def halo_copy(sweep, block):
        return pltpu.make_async_remote_copy(
            src_ref=halo_send.at[sweep, block],
            dst_ref=ghost.at[sweep, block],
            send_sem=halo_send_sem.at[sweep, block],
            recv_sem=halo_recv_sem.at[sweep, block],
            device_id=(lax.rem(me_dom + OFFSETS[block] + pn.dom, pn.dom), me_rep),
            device_id_type=MESH,
        )

    def send_halo(sweep):
        for block in range(4):
            for half in range(pn.halo_chunks):
                found = pick(field, 0, n_ch, wide_row(send_ref, block, half), zeros)
                for g in range(groups):
                    halo_send[sweep, block, half * rpad + g * 8 : half * rpad + g * 8 + 8, :] = found[g]
            halo_copy(sweep, block).start()

    def beside_at(face, tile, g):
        count = min(8, rows - g * 8)
        return pl.ds((face * rows + g * 8) * n_ch + tile, count, stride=n_ch), count

    n_faces = neighbor_ref.shape[0]

    def gather_local():
        def body(face, tile, carry):
            found = pick(field, 0, n_ch, wide_row(neighbor_ref, face, tile), zeros)
            for g in range(groups):
                where, count = beside_at(face, tile, g)
                beside[where, :] = found[g][:count]
            return carry

        for face in range(n_faces):
            lax.fori_loop(0, n_ch, functools.partial(body, face), 0)

    def gather_ghost(sweep):
        for block in range(4):
            halo_copy(sweep, block).wait()

        def body(face, tile, carry):
            start = []
            for g in range(groups):
                where, count = beside_at(face, tile, g)
                value = beside[where, :]
                if count < 8:
                    value = jnp.concatenate([value, jnp.zeros((8 - count, LANES), F32)], axis=0)
                start.append(value)
            index = wide_row(neighbor_ref, face, tile)
            for block in range(4):
                start = pick(
                    ghost.at[sweep, block], n_ch + block * pn.halo_chunks, pn.halo_chunks, index, start
                )
            for g in range(groups):
                where, count = beside_at(face, tile, g)
                beside[where, :] = start[g][:count]
            return carry

        for face in range(n_faces):
            lax.fori_loop(0, n_ch, functools.partial(body, face), 0)

    def line(ref, index):
        return ref[pl.ds(pl.multiple_of(index * n_ch, n_ch), n_ch), :]

    def couple():
        def body(e, carry):
            total = [jnp.zeros((n_ch, LANES), F32)] * width
            for face in range(n_faces):
                for g in range(pn.comps):
                    entry = line(jac, (face * pn.comps + e) * pn.comps + g)
                    for k in range(width):
                        total[k] = total[k] + entry * line(beside, face * rows + g * width + k)
            for k in range(width):
                coupled[pl.ds(pl.multiple_of((e * width + k) * n_ch, n_ch), n_ch), :] = total[k]
            return carry

        lax.fori_loop(0, pn.comps, body, 0)

    def update():
        own = [freq_ref[me_rep * pn.pairs + p] for p in range(pn.pairs)]
        for k in range(width):
            part, pair = k // pn.pairs, k % pn.pairs
            turned = (1 - part) * pn.pairs + pair
            sign = own[pair] if part == 0 else -own[pair]
            residual = []
            for g in range(pn.comps):
                row = g * width + k
                residual.append(
                    line(flow, row) - line(coupled, row) + sign * line(iterate, g * width + turned)
                )
            for e in range(pn.comps):
                total = line(diag, e * pn.comps) * residual[0]
                for g in range(1, pn.comps):
                    total = total + line(diag, e * pn.comps + g) * residual[g]
                row = e * width + k
                coupled[row * n_ch : (row + 1) * n_ch, :] = total
        for row in range(rows):
            iterate[row * n_ch : (row + 1) * n_ch, :] = line(coupled, row)

    for e in range(pn.comps):
        for r in range(2):
            unfold(prev_ref[e, r], iterate, (e * width + r * pn.pairs) * n_ch)
    spread_field()
    send_halo(0)

    for offset in range(1, pn.rep):
        rep_copy(offset).wait()

    per = 4 if lines % 4 == 0 else 1
    n_slot = pn.dom * pn.slot_rows
    pack_flat = pack_buf
    for d in range(pn.dom):
        pack_buf[d] = jnp.zeros((pn.slot_rows, pn.width), F32)

    def pack(turn, carry):
        for c in range(per):
            chunk = turn * per + c
            lanes = slice(c * LANES, (c + 1) * LANES)
            slot = slot_buf[pl.ds(chunk, 1), :]
            owner = chunk // pn.blocks
            column = pl.multiple_of(chunk % pn.blocks * LANES, LANES)
            value = face_buf[owner, :, pl.ds(column, LANES)]
            cell = cell_ref[pl.ds(chunk, 1), :].astype(F32)
            low = jnp.broadcast_to(slot % pn.width, (pn.width, LANES))
            right_buf[:, lanes] = jnp.where(low == iota((pn.width, LANES), 0), 1.0, 0.0).astype(BF16)
            high = jnp.broadcast_to(slot // pn.width, (8, LANES))
            sub = iota((8, LANES), 0)
            tiles = []
            for tile in range(pn.slot_rows // 8):
                row = jnp.zeros((8, LANES), F32)
                for v in range(pn.values + 1):
                    source = value[v : v + 1] if v < pn.values else cell
                    low_row, top_row = v * pn.steps - tile * 8, (v + 1) * pn.steps - tile * 8
                    if top_row <= 0 or low_row >= 8:
                        continue
                    inside = (sub >= low_row) & (sub < top_row)
                    row = jnp.where(inside, jnp.broadcast_to(source, (8, LANES)), row)
                tiles.append(row)
            parts = [split(t) for t in tiles]
            parts = [(a.astype(F32), b.astype(F32)) for a, b in parts]
            halves = ([], [])
            for d in range(pn.dom):
                for tile in range(pn.slot_rows // 8):
                    step = (sub + tile * 8) % pn.steps
                    here = high == d * pn.steps + step
                    for half in range(2):
                        halves[half].append(jnp.where(here, parts[tile][half], 0.0))
            left_buf[0:n_slot, lanes] = jnp.concatenate(halves[0], axis=0).astype(BF16)
            left_buf[n_slot : 2 * n_slot, lanes] = jnp.concatenate(halves[1], axis=0).astype(BF16)
        found = dot_last(left_buf[...], right_buf[...])
        for d in range(pn.dom):
            a, b = d * pn.slot_rows, n_slot + d * pn.slot_rows
            pack_buf[d] += found[a : a + pn.slot_rows] + found[b : b + pn.slot_rows]
        return carry

    lax.fori_loop(0, lines // per, pack, 0)

    def dom_copy(offset):
        target = lax.rem(me_dom + offset, pn.dom)
        return pltpu.make_async_remote_copy(
            src_ref=pack_buf.at[target],
            dst_ref=recv_buf.at[offset],
            send_sem=dom_send_sem.at[offset],
            recv_sem=dom_recv_sem.at[offset],
            device_id=(target, me_rep),
            device_id_type=MESH,
        )

    def send_faces(offset, carry):
        dom_copy(offset).start()
        return carry

    lax.fori_loop(1, pn.dom, send_faces, 0)
    recv_buf[0] = pack_buf[me_dom]

    def unfold_jac(index, carry):
        unfold(jac_ref[index].astype(F32), jac, index * (pn.comps * n_ch))
        return carry

    lax.fori_loop(0, n_faces * pn.comps, unfold_jac, 0)
    for e in range(pn.comps):
        unfold(diag_ref[e], diag, e * pn.comps * n_ch)
        unfold(weight_ref[e], weight, e * 2 * n_ch)
        for r in range(2):
            unfold(flow_ref[e, r], flow, (e * width + r * pn.pairs) * n_ch)
    gather_local()
    gather_ghost(0)
    couple()

    wall_buf[...] = jnp.zeros(wall_buf.shape, F32)
    half_rows = pn.values * n_ch

    def add_faces(offset):
        for step in range(pn.steps):
            for part in range(pn.width // LANES):
                place = step * pn.width + part * LANES
                lanes = slice(part * LANES, (part + 1) * LANES)
                row = pn.values * pn.steps + step
                cell = recv_buf[offset, row : row + 1, lanes].astype(jnp.int32)
                low = jnp.broadcast_to(cell % LANES, (LANES, LANES))
                add_right[:, place : place + LANES] = jnp.where(
                    low == iota((LANES, LANES), 0), 1.0, 0.0
                ).astype(BF16)
                here = jnp.broadcast_to(cell // LANES, (n_ch, LANES)) == iota((n_ch, LANES), 0)
                for v in range(pn.values):
                    row = v * pn.steps + step
                    value = jnp.broadcast_to(recv_buf[offset, row : row + 1, lanes], (n_ch, LANES))
                    first, second = split(jnp.where(here, value, 0.0))
                    add_left[v * n_ch : (v + 1) * n_ch, place : place + LANES] = first
                    add_left[
                        half_rows + v * n_ch : half_rows + (v + 1) * n_ch, place : place + LANES
                    ] = second
        found = dot_last(add_left[...], add_right[...])
        wall_buf[...] += found[:half_rows] + found[half_rows:]

    add_faces(0)

    def receive(offset, carry):
        dom_copy(offset).wait()
        add_faces(offset)
        return carry

    lax.fori_loop(1, pn.dom, receive, 0)

    for e in range(pn.comps):
        first, second = line(weight, 2 * e), line(weight, 2 * e + 1)
        for k in range(width):
            row = e * width + k
            flow[row * n_ch : (row + 1) * n_ch, :] = (
                line(flow, row) + first * line(wall_buf, k) + second * line(wall_buf, width + k)
            )

    update()
    for sweep in range(1, SWEEPS):
        spread_field()
        send_halo(sweep)
        gather_local()
        gather_ghost(sweep)
        couple()
        update()

    for e in range(pn.comps):
        for r in range(2):
            for tile in range(n_ch):
                start = (e * width + r * pn.pairs) * n_ch + tile
                out_ref[e, r, :, tile * LANES : (tile + 1) * LANES] = iterate[
                    pl.ds(start, pn.pairs, stride=n_ch), :
                ]


def shards(
    dom,
    rep,
    spline_blocks,
    modal_coeff,
    frequency,
    face_dest,
    face_cell,
    wall_weight,
    flow_rhs,
    previous,
    diag_inverse,
    off_jacobian,
    neighbor,
    send_list,
):
    pn = Plan(dom, rep, spline_blocks, face_dest, flow_rhs, send_list)
    modes = modal_coeff.shape[0]
    turned = jnp.transpose(modal_coeff.reshape(modes, 2, rep, pn.pairs), (2, 1, 3, 0))
    both = jnp.stack([turned[:, ::-1], turned], axis=1)
    same = jnp.eye(2, dtype=BF16)[None, :, None, None, :, None]
    coeff = (both[:, :, :, :, None, :] * same).reshape(rep * pn.values, 2 * modes)
    n_faces = neighbor.shape[0]
    lines = pn.face_chunks
    per = 4 if lines % 4 == 0 else 1
    vmem = pl.BlockSpec(memory_space=pltpu.VMEM)
    return pl.pallas_call(
        functools.partial(kernel, pn),
        out_shape=jax.ShapeDtypeStruct(previous.shape, F32),
        in_specs=[pl.BlockSpec(memory_space=pltpu.SMEM)] + [vmem] * 11,
        out_specs=vmem,
        scratch_shapes=[
            pltpu.VMEM((rep, pn.values, pn.own_faces), F32),
            pltpu.VMEM((rep, pn.values, pn.own_faces), F32),
            pltpu.VMEM((lines, LANES), jnp.int32),
            pltpu.VMEM((2 * dom * pn.slot_rows, per * LANES), BF16),
            pltpu.VMEM((pn.width, per * LANES), BF16),
            pltpu.VMEM((dom, pn.slot_rows, pn.width), F32),
            pltpu.VMEM((dom, pn.slot_rows, pn.width), F32),
            pltpu.VMEM((2 * pn.values * pn.chunks, pn.cap), BF16),
            pltpu.VMEM((LANES, pn.cap), BF16),
            pltpu.VMEM((pn.values * pn.chunks, LANES), F32),
            pltpu.VMEM((pn.chunks * pn.row_pad, LANES), F32),
            pltpu.VMEM((SWEEPS, 4, pn.halo_chunks * pn.row_pad, LANES), F32),
            pltpu.VMEM((SWEEPS, 4, pn.halo_chunks * pn.row_pad, LANES), F32),
            pltpu.VMEM((n_faces * pn.rows * pn.chunks, LANES), F32),
            pltpu.VMEM((n_faces * pn.comps * pn.comps * pn.chunks, LANES), F32),
            pltpu.VMEM((pn.comps * pn.comps * pn.chunks, LANES), F32),
            pltpu.VMEM((pn.comps * 2 * pn.chunks, LANES), F32),
            pltpu.VMEM((pn.rows * pn.chunks, LANES), F32),
            pltpu.VMEM((pn.rows * pn.chunks, LANES), F32),
            pltpu.VMEM((pn.rows * pn.chunks, LANES), F32),
            pltpu.SemaphoreType.DMA((rep,)),
            pltpu.SemaphoreType.DMA((rep,)),
            pltpu.SemaphoreType.DMA((dom,)),
            pltpu.SemaphoreType.DMA((dom,)),
            pltpu.SemaphoreType.DMA((SWEEPS, 4)),
            pltpu.SemaphoreType.DMA((SWEEPS, 4)),
        ],
        compiler_params=pltpu.CompilerParams(
            collective_id=0, has_side_effects=True, vmem_limit_bytes=48 * 1024 * 1024
        ),
    )(
        frequency,
        spline_blocks.reshape(pn.blocks, 2 * modes, LANES),
        coeff,
        face_dest.reshape(lines, LANES),
        face_cell.reshape(lines, LANES),
        wall_weight,
        flow_rhs,
        previous,
        diag_inverse,
        off_jacobian.reshape(n_faces * pn.comps, pn.comps, pn.cells),
        neighbor,
        send_list,
    )


def solution(mesh):
    return jax.shard_map(
        functools.partial(shards, mesh.shape["dom"], mesh.shape["rep"]),
        mesh=mesh,
        in_specs=(
            P(("dom", "rep"), None, None, None),
            P(),
            P(),
            P("dom", None),
            P("dom"),
            P(None, None, "dom"),
            P(None, None, "rep", "dom"),
            P(None, None, "rep", "dom"),
            P(None, None, "dom"),
            P(None, None, None, "dom"),
            P(None, "dom"),
            P(None, "dom"),
        ),
        out_specs=P(None, None, "rep", "dom"),
        check_vma=False,
    )
```

time: 309 us -> 71 us (0.23)
  local copies, waits for them, and re-layouts: 172 us -> 3.63 us
  other arithmetic: 78.8 us -> 0.09 us
  Pallas kernels: 0 us -> 66.9 us
  starting transfers between devices: 28.2 us -> 0 us
  between operations: 14.1 us -> 0.15 us
  waiting for transfers between devices: 11.1 us -> 0 us
    gather x4 -> x0, local copies, waits for them, and re-layouts: 99 us -> none  [the longest x2 90.6 us: shards(): jnp.take(extended, neighbor_flat, axis=1)]
    pallas_call x0 -> x1, Pallas kernels: none -> 66.9 us  [shards(): pl.pallas_call(functools.partial(kernel, pn), out_shape=jax.ShapeDtypeStr...]
    scatter-add x1 -> x0, other arithmetic: 44.6 us -> none  [shards(): wall_sum = jnp.zeros((4 * pair_dev, cell_count), jnp.float32).at[:, cell_...]
    select_n x6 -> x0, other arithmetic: 22.2 us -> none  [the longest x2 20.7 us: shards(): jnp.take(extended, neighbor_flat, axis=1)]
    unnamed x60 -> x24, local copies, waits for them, and re-layouts: 22 us -> 3.54 us
    ppermute x8 -> x0, starting transfers between devices: 18.4 us -> none  [from_behind(): lax.ppermute(value, axis, [(i, (i + by) % length) for i in range(length)])]
    scatter x1 -> x0, local copies, waits for them, and re-layouts: 13.1 us -> none  [shards(): jnp.zeros((4 * pair_dev, dom_size * capacity), jnp.float32).at[:, slot_flat]]
    reshape x13 -> x0, local copies, waits for them, and re-layouts: 12.5 us -> none  [the longest x1 3.45 us: shards(): send_values.reshape(4 * pair_dev, dom_size, capacity)]
  transfers between devices with their start and end apart: 11 -> 0, of which waited for: 2 -> 0; matrix products, arithmetic and copies ran while one was open for 32% -> 0% of each run, Pallas kernels for 0% -> 0%
where the time goes in v1:
time: 71 us; the launch traced here: 70.8 us
  Pallas kernels  66.9 us (94%)
  local copies, waits for them, and re-layouts  3.63 us (5%)
    pallas_call x1, Pallas kernels, shards(): pl.pallas_call(functools.partial(kernel, pn), out_shape=jax.ShapeDtypeStr...  66.9 us
    unnamed x24, local copies, waits for them, and re-layouts  3.54 us

profile of v1, /device:TPU:0, one launch (start us, length us, event | category | flops | bytes accessed | tf_op | source)
XLA Modules:
  0.0 70.8 jit_solution(11794598193009568027)
XLA Ops:
  0.0 0.0 copy-start.10
  0.0 0.7 copy-done.10
  0.7 0.1 broadcast_multiply_fusion
  0.8 0.1 mul.20.coeff_ref
  0.9 0.0 copy-start
  0.9 0.0 copy-start.1
  0.9 0.0 copy-start.2
  0.9 0.0 copy-start.3
  0.9 0.0 copy-start.4
  0.9 0.0 copy-start.5
  0.9 0.0 copy-start.6
  0.9 0.0 copy-start.7
  0.9 0.0 copy-start.8
  1.0 1.6 %copy.14 = bf16[6,5,5,2048]{3,2,1,0:T(8,128)(2,1)S(1)} copy(bf16[6,5,5,2048]{3,0,2,1:T(8,128)(2,1)} %param.21) | data formatting | bytes 1228800 | tf_op args[9]
  2.5 0.0 copy-start.9
  2.5 0.0 copy-done
  2.6 0.0 copy-done.1
  2.6 0.0 copy-done.2
  2.6 0.0 copy-done.3
  2.6 0.0 copy-done.4
  2.6 0.0 copy-done.5
  2.6 0.0 copy-done.6
  2.6 0.0 copy-done.7
  2.6 0.0 copy-done.8
  2.6 0.6 copy-done.9
  3.2 66.9 %shard_map.118 = f32[5,2,2,2048]{3,2,1,0:T(2,128)S(1)} custom-call(f32[8]{0:T(128)S(1)} %copy-done.9, bf16[8,128,128]{2,1,0:T(8,128)(2,1)S(1)} %bitcast.12, bf16[32,128]{1,0:T(8,128)(2,1)S(1)} %mul.20.coeff_ref, s32[32,128]{1,0:T(8,128)S(1)} %bitcast.13, s32[32,128]{1,0:T(8,128)S(1)} %bitcast.14, f32[5,2,2048]{2,1,0:T(2,128)S(1)} %copy-done.4, ...), custom_call_target="tpu_custom_call" | custom-call | tf_op jit(solution)/shard_map/pallas_call | solution.py:482
  70.1 0.7 copy.18
  (2 shorter events, 0.0 us)
Async XLA Ops:
  0.0 0.7 copy-start.10
  0.9 1.7 %copy-start = (f32[5,5,2048]{2,1,0:T(8,128)S(1)}, f32[5,5,2048]{2,1,0:T(8,128)}, u32[]{:S(2)}) copy-start(f32[5,5,2048]{2,1,0:T(8,128)} %diag_ref.1) | copy-start | bytes 614404
  0.9 1.7 %copy-start.1 = (bf16[8,2,64,128]{3,2,1,0:T(8,128)(2,1)S(1)}, bf16[8,2,64,128]{3,2,1,0:T(8,128)(2,1)}, u32[]{:S(2)}) copy-start(bf16[8,2,64,128]{3,2,1,0:T(8,128)(2,1)} %param.12) | copy-start | bytes 786436
  0.9 1.7 %copy-start.2 = (f32[5,2,2,2048]{3,2,1,0:T(2,128)S(1)}, f32[5,2,2,2048]{3,2,1,0:T(2,128)}, u32[]{:S(2)}) copy-start(f32[5,2,2,2048]{3,2,1,0:T(2,128)} %flow_ref.1) | copy-start | bytes 491524
  0.9 1.7 %copy-start.3 = (f32[5,2,2,2048]{3,2,1,0:T(2,128)S(1)}, f32[5,2,2,2048]{3,2,1,0:T(2,128)}, u32[]{:S(2)}) copy-start(f32[5,2,2,2048]{3,2,1,0:T(2,128)} %prev_ref.1) | copy-start | bytes 491524
  0.9 1.7 %copy-start.4 = (f32[5,2,2048]{2,1,0:T(2,128)S(1)}, f32[5,2,2048]{2,1,0:T(2,128)}, u32[]{:S(2)}) copy-start(f32[5,2,2048]{2,1,0:T(2,128)} %weight_ref.1) | copy-start | bytes 245764
  0.9 1.7 %copy-start.5 = (s32[6,2048]{1,0:T(8,128)S(1)}, s32[6,2048]{1,0:T(8,128)}, u32[]{:S(2)}) copy-start(s32[6,2048]{1,0:T(8,128)} %neighbor_ref.1) | copy-start | bytes 147460
  0.9 1.7 %copy-start.6 = (s32[4096,1]{0,1:T(1,128)S(1)}, s32[4096,1]{0,1:T(1,128)}, u32[]{:S(2)}) copy-start(s32[4096,1]{0,1:T(1,128)} %param.15) | copy-start | bytes 49156
  0.9 1.7 %copy-start.7 = (s32[4096]{0:T(1024)S(1)}, s32[4096]{0:T(1024)}, u32[]{:S(2)}) copy-start(s32[4096]{0:T(1024)} %param.16) | copy-start | bytes 49156
  0.9 1.7 %copy-start.8 = (s32[4,256]{1,0:T(4,128)S(1)}, s32[4,256]{1,0:T(4,128)}, u32[]{:S(2)}) copy-start(s32[4,256]{1,0:T(4,128)} %send_ref.1) | copy-start | bytes 12292
  2.5 0.7 copy-start.9

commit v2 on v1

--- a/solution.py
+++ b/solution.py
@@ -19,6 +19,14 @@
     return lax.broadcasted_iota(jnp.int32, shape, axis)
 
 
+def remainder(value, size):
+    return value & (size - 1) if size & (size - 1) == 0 else value % size
+
+
+def quotient(value, size):
+    return value >> (size.bit_length() - 1) if size & (size - 1) == 0 else value // size
+
+
 def split(value):
     high = value.astype(BF16)
     return high, (value - high.astype(F32)).astype(BF16)
@@ -26,10 +34,6 @@
 
 def dot_last(a, b):
     return lax.dot_general(a, b, (((1,), (1,)), ((), ())), preferred_element_type=F32)
-
-
-def lane_pick(table, index):
-    return jnp.take_along_axis(table, index, axis=1, mode="promise_in_bounds")
 
 
 class Plan:
@@ -54,7 +58,7 @@
             count += 1
         self.slot_rows = count * self.steps
         self.chunks = self.cells // LANES
-        self.halo_chunks = self.halo // LANES
+        self.wide = min(2 * LANES, self.halo)
         self.face_chunks = self.faces // LANES
 
 
@@ -84,6 +88,12 @@
     add_right,
     wall_buf,
     field,
+    table,
+    table_far,
+    hot_send,
+    hot_near,
+    high_buf,
+    near,
     ghost,
     halo_send,
     beside,
@@ -184,25 +194,46 @@
                 :, tile * LANES : (tile + 1) * LANES
             ]
 
+    wide, n_wide = pn.wide, pn.cells // pn.wide
+    per_wide = wide // LANES
+    n_faces = neighbor_ref.shape[0]
+
     def spread_field():
         for row in range(rows):
             field[pl.ds(row, n_ch, stride=rpad), :] = iterate[row * n_ch : (row + 1) * n_ch]
-
-    def pick(table, first_chunk, count, index, start):
-        low, high = index % LANES, index // LANES
+        blocks = [
+            jnp.concatenate(
+                [
+                    field[chunk * rpad : (chunk + 1) * rpad, :]
+                    for chunk in range(c * per_wide, (c + 1) * per_wide)
+                ],
+                axis=1,
+            )
+            for c in range(n_wide)
+        ]
+        table[:, :wide], table[:, wide:] = split(jnp.concatenate(blocks, axis=0))
+
+    def pick(parts, first_chunk, count, hot, high, start):
+        found = jnp.dot(parts, jnp.concatenate([hot, hot], axis=0), preferred_element_type=F32)
         picked = list(start)
         for chunk in range(count):
             here = high == first_chunk + chunk
             for g in range(groups):
-                found = lane_pick(table[pl.ds(chunk * rpad + g * 8, 8), :], low)
-                picked[g] = jnp.where(here, found, picked[g])
+                at = chunk * rpad + g * 8
+                picked[g] = jnp.where(here, found[at : at + 8], picked[g])
         return picked
 
-    def wide_row(ref, row, tile):
-        line = ref[row : row + 1, pl.ds(pl.multiple_of(tile * LANES, LANES), LANES)]
-        return jnp.broadcast_to(line, (8, LANES))
-
-    zeros = [jnp.zeros((8, LANES), F32)] * groups
+    def one_hot(low, target):
+        both = jnp.concatenate([low, low], axis=0)
+
+        def body(turn, carry):
+            first = pl.multiple_of(turn * 16, 16)
+            target[pl.ds(first, 16), :] = jnp.where(
+                both == iota(both.shape, 0) + first, 1.0, 0.0
+            ).astype(BF16)
+            return carry
+
+        lax.fori_loop(0, wide // 16, body, 0)
 
     def halo_copy(sweep, block):
         return pltpu.make_async_remote_copy(
@@ -216,53 +247,46 @@
 
     def send_halo(sweep):
         for block in range(4):
-            for half in range(pn.halo_chunks):
-                found = pick(field, 0, n_ch, wide_row(send_ref, block, half), zeros)
-                for g in range(groups):
-                    halo_send[sweep, block, half * rpad + g * 8 : half * rpad + g * 8 + 8, :] = found[g]
+            index = jnp.broadcast_to(send_ref[block : block + 1, :], (8, pn.halo))
+            zeros = [jnp.zeros((8, pn.halo), F32)] * groups
+            found = pick(table[...], 0, n_wide, hot_send[block], quotient(index, wide), zeros)
+            for g in range(groups):
+                halo_send[sweep, block, g * 8 : g * 8 + 8, :] = found[g]
             halo_copy(sweep, block).start()
 
-    def beside_at(face, tile, g):
-        count = min(8, rows - g * 8)
-        return pl.ds((face * rows + g * 8) * n_ch + tile, count, stride=n_ch), count
-
-    n_faces = neighbor_ref.shape[0]
-
     def gather_local():
-        def body(face, tile, carry):
-            found = pick(field, 0, n_ch, wide_row(neighbor_ref, face, tile), zeros)
+        def body(face, carry):
+            high = high_buf[face]
+            zeros = [jnp.zeros(high.shape, F32)] * groups
+            found = pick(table[...], 0, n_wide, hot_near[face], high, zeros)
             for g in range(groups):
-                where, count = beside_at(face, tile, g)
-                beside[where, :] = found[g][:count]
+                near[face, g * 8 : g * 8 + 8, :] = found[g]
             return carry
 
-        for face in range(n_faces):
-            lax.fori_loop(0, n_ch, functools.partial(body, face), 0)
+        lax.fori_loop(0, n_faces, body, 0)
+
+    n_ghost = pn.halo // wide
 
     def gather_ghost(sweep):
         for block in range(4):
             halo_copy(sweep, block).wait()
-
-        def body(face, tile, carry):
-            start = []
+        blocks = []
+        for chunk in range(4 * n_ghost):
+            lane = chunk % n_ghost * wide
+            blocks.append(ghost[sweep, chunk // n_ghost, :, lane : lane + wide])
+        table_far[:, :wide], table_far[:, wide:] = split(jnp.concatenate(blocks, axis=0))
+
+        def body(face, carry):
+            start = [near[face, g * 8 : g * 8 + 8, :] for g in range(groups)]
+            found = pick(table_far[...], n_wide, 4 * n_ghost, hot_near[face], high_buf[face], start)
             for g in range(groups):
-                where, count = beside_at(face, tile, g)
-                value = beside[where, :]
-                if count < 8:
-                    value = jnp.concatenate([value, jnp.zeros((8 - count, LANES), F32)], axis=0)
-                start.append(value)
-            index = wide_row(neighbor_ref, face, tile)
-            for block in range(4):
-                start = pick(
-                    ghost.at[sweep, block], n_ch + block * pn.halo_chunks, pn.halo_chunks, index, start
-                )
-            for g in range(groups):
-                where, count = beside_at(face, tile, g)
-                beside[where, :] = start[g][:count]
+                count = min(8, rows - g * 8)
+                for tile in range(n_ch):
+                    where = pl.ds((face * rows + g * 8) * n_ch + tile, count, stride=n_ch)
+                    beside[where, :] = found[g][:count, tile * LANES : (tile + 1) * LANES]
             return carry
 
-        for face in range(n_faces):
-            lax.fori_loop(0, n_ch, functools.partial(body, face), 0)
+        lax.fori_loop(0, n_faces, body, 0)
 
     def line(ref, index):
         return ref[pl.ds(pl.multiple_of(index * n_ch, n_ch), n_ch), :]
@@ -272,7 +296,7 @@
             total = [jnp.zeros((n_ch, LANES), F32)] * width
             for face in range(n_faces):
                 for g in range(pn.comps):
-                    entry = line(jac, (face * pn.comps + e) * pn.comps + g)
+                    entry = line(jac, (e * pn.comps + g) * n_faces + face)
                     for k in range(width):
                         total[k] = total[k] + entry * line(beside, face * rows + g * width + k)
             for k in range(width):
@@ -305,15 +329,18 @@
     for e in range(pn.comps):
         for r in range(2):
             unfold(prev_ref[e, r], iterate, (e * width + r * pn.pairs) * n_ch)
+    field[...] = jnp.zeros(field.shape, F32)
     spread_field()
+    for block in range(4):
+        index = jnp.broadcast_to(send_ref[block : block + 1, :], (8, pn.halo))
+        one_hot(remainder(index, wide), hot_send.at[block])
     send_halo(0)
 
     for offset in range(1, pn.rep):
         rep_copy(offset).wait()
 
-    per = 4 if lines % 4 == 0 else 1
+    per = 8 if lines % 8 == 0 else 1
     n_slot = pn.dom * pn.slot_rows
-    pack_flat = pack_buf
     for d in range(pn.dom):
         pack_buf[d] = jnp.zeros((pn.slot_rows, pn.width), F32)
 
@@ -326,9 +353,9 @@
             column = pl.multiple_of(chunk % pn.blocks * LANES, LANES)
             value = face_buf[owner, :, pl.ds(column, LANES)]
             cell = cell_ref[pl.ds(chunk, 1), :].astype(F32)
-            low = jnp.broadcast_to(slot % pn.width, (pn.width, LANES))
+            low = jnp.broadcast_to(remainder(slot, pn.width), (pn.width, LANES))
             right_buf[:, lanes] = jnp.where(low == iota((pn.width, LANES), 0), 1.0, 0.0).astype(BF16)
-            high = jnp.broadcast_to(slot // pn.width, (8, LANES))
+            high = jnp.broadcast_to(quotient(slot, pn.width), (8, LANES))
             sub = iota((8, LANES), 0)
             tiles = []
             for tile in range(pn.slot_rows // 8):
@@ -346,7 +373,7 @@
             halves = ([], [])
             for d in range(pn.dom):
                 for tile in range(pn.slot_rows // 8):
-                    step = (sub + tile * 8) % pn.steps
+                    step = remainder(sub + tile * 8, pn.steps)
                     here = high == d * pn.steps + step
                     for half in range(2):
                         halves[half].append(jnp.where(here, parts[tile][half], 0.0))
@@ -379,10 +406,14 @@
     recv_buf[0] = pack_buf[me_dom]
 
     def unfold_jac(index, carry):
-        unfold(jac_ref[index].astype(F32), jac, index * (pn.comps * n_ch))
+        unfold(jac_ref[index].astype(F32), jac, index * (n_faces * n_ch))
         return carry
 
-    lax.fori_loop(0, n_faces * pn.comps, unfold_jac, 0)
+    lax.fori_loop(0, pn.comps * pn.comps, unfold_jac, 0)
+    for face in range(n_faces):
+        index = jnp.broadcast_to(neighbor_ref[face : face + 1, :], (8, pn.cells))
+        high_buf[face] = quotient(index, wide)
+        one_hot(remainder(index, wide), hot_near.at[face])
     for e in range(pn.comps):
         unfold(diag_ref[e], diag, e * pn.comps * n_ch)
         unfold(weight_ref[e], weight, e * 2 * n_ch)
@@ -402,11 +433,11 @@
                 lanes = slice(part * LANES, (part + 1) * LANES)
                 row = pn.values * pn.steps + step
                 cell = recv_buf[offset, row : row + 1, lanes].astype(jnp.int32)
-                low = jnp.broadcast_to(cell % LANES, (LANES, LANES))
+                low = jnp.broadcast_to(remainder(cell, LANES), (LANES, LANES))
                 add_right[:, place : place + LANES] = jnp.where(
                     low == iota((LANES, LANES), 0), 1.0, 0.0
                 ).astype(BF16)
-                here = jnp.broadcast_to(cell // LANES, (n_ch, LANES)) == iota((n_ch, LANES), 0)
+                here = jnp.broadcast_to(quotient(cell, LANES), (n_ch, LANES)) == iota((n_ch, LANES), 0)
                 for v in range(pn.values):
                     row = v * pn.steps + step
                     value = jnp.broadcast_to(recv_buf[offset, row : row + 1, lanes], (n_ch, LANES))
@@ -477,7 +508,7 @@
     coeff = (both[:, :, :, :, None, :] * same).reshape(rep * pn.values, 2 * modes)
     n_faces = neighbor.shape[0]
     lines = pn.face_chunks
-    per = 4 if lines % 4 == 0 else 1
+    per = 8 if lines % 8 == 0 else 1
     vmem = pl.BlockSpec(memory_space=pltpu.VMEM)
     return pl.pallas_call(
         functools.partial(kernel, pn),
@@ -496,8 +527,14 @@
             pltpu.VMEM((LANES, pn.cap), BF16),
             pltpu.VMEM((pn.values * pn.chunks, LANES), F32),
             pltpu.VMEM((pn.chunks * pn.row_pad, LANES), F32),
-            pltpu.VMEM((SWEEPS, 4, pn.halo_chunks * pn.row_pad, LANES), F32),
-            pltpu.VMEM((SWEEPS, 4, pn.halo_chunks * pn.row_pad, LANES), F32),
+            pltpu.VMEM((pn.cells // pn.wide * pn.row_pad, 2 * pn.wide), BF16),
+            pltpu.VMEM((4 * pn.halo // pn.wide * pn.row_pad, 2 * pn.wide), BF16),
+            pltpu.VMEM((4, pn.wide, pn.halo), BF16),
+            pltpu.VMEM((n_faces, pn.wide, pn.cells), BF16),
+            pltpu.VMEM((n_faces, 8, pn.cells), jnp.int32),
+            pltpu.VMEM((n_faces, pn.row_pad, pn.cells), F32),
+            pltpu.VMEM((SWEEPS, 4, pn.row_pad, pn.halo), F32),
+            pltpu.VMEM((SWEEPS, 4, pn.row_pad, pn.halo), F32),
             pltpu.VMEM((n_faces * pn.rows * pn.chunks, LANES), F32),
             pltpu.VMEM((n_faces * pn.comps * pn.comps * pn.chunks, LANES), F32),
             pltpu.VMEM((pn.comps * pn.comps * pn.chunks, LANES), F32),
@@ -525,7 +562,7 @@
         flow_rhs,
         previous,
         diag_inverse,
-        off_jacobian.reshape(n_faces * pn.comps, pn.comps, pn.cells),
+        jnp.transpose(off_jacobian, (1, 2, 0, 3)).reshape(pn.comps * pn.comps, n_faces, pn.cells),
         neighbor,
         send_list,
     )

time: 71 us -> 45 us (0.63)
  Pallas kernels: 66.9 us -> 34.4 us
  local copies, waits for them, and re-layouts: 3.63 us -> 9.29 us
    pallas_call x1, Pallas kernels: 66.9 us -> 34.4 us  [shards(): pl.pallas_call(functools.partial(kernel, pn), out_shape=jax.ShapeDtypeStr...]
    unnamed x24 -> x23, local copies, waits for them, and re-layouts: 3.54 us -> 8.48 us
    another operation x1, local copies, waits for them, and re-layouts: 0.01 us -> 0.72 us  [shards(): both = jnp.stack([turned[:, ::-1], turned], axis=1)]
where the time goes in v2:
time: 45 us; the launch traced here: 44.5 us
  Pallas kernels  34.4 us (76%)
  local copies, waits for them, and re-layouts  9.29 us (21%)
  other arithmetic  0.77 us (2%)
    pallas_call x1, Pallas kernels, shards(): pl.pallas_call(functools.partial(kernel, pn), out_shape=jax.ShapeDtypeStr...  34.4 us
    unnamed x23, local copies, waits for them, and re-layouts  8.48 us

profile of v2, /device:TPU:0, one launch (start us, length us, event | category | flops | bytes accessed | tf_op | source)
XLA Modules:
  0.0 44.5 jit_solution(7842987169708238208)
XLA Ops:
  0.0 0.0 copy-start.6
  0.0 0.7 %reverse_bitcast_fusion = bf16[4,1,2,2,64]{4,3,0,2,1:T(2,128)(2,1)S(1)} fusion(bf16[4,2,2,64]{3,2,0,1:T(2,128)(2,1)} %bitcast.17), kind=kLoop, calls=%fused_computation.2 | loop fusion | bytes 4096 | tf_op jit(solution)/shard_map/stack | solution.py:506
  0.7 0.8 %broadcast_multiply_fusion = bf16[4,2,2,2,2,64]{5,4,3,2,1,0:T(2,128)(2,1)S(1)} fusion(bf16[2,2]{1,0:T(2,128)(2,1)S(1)} %compare_convert_fusion, bf16[4,1,2,2,64]{4,3,0,2,1:T(2,128)(2,1)} %bitcast.18, bf16[4,1,2,2,64]{4,3,0,2,1:T(2,128)(2,1)S(1)} %reverse_bitcast_fusion), kind=kLoop, calls=%fused_computation.1 | loop fusion | flops 18432 | bytes 12296 | tf_op jit(solution)/shard_map/mul | solution.py:508
  1.5 0.0 copy-start.9
  1.5 0.0 copy-start.10
  1.5 0.1 mul.20.coeff_ref
  1.6 0.0 copy-done.6
  1.6 0.6 %copy-done.9 = s32[4,256]{1,0:T(4,128)S(1)} copy-done((s32[4,256]{1,0:T(4,128)S(1)}, s32[4,256]{1,0:T(4,128)}, u32[]{:S(2)}) %copy-start.9) | copy-done | bytes 4120
  2.2 0.0 copy-done.10
  2.2 0.0 copy-start
  2.2 1.1 %copy-done = bf16[6,5,5,2048]{3,0,2,1:T(8,128)(2,1)S(1)} copy-done((bf16[6,5,5,2048]{3,0,2,1:T(8,128)(2,1)S(1)}, bf16[6,5,5,2048]{3,0,2,1:T(8,128)(2,1)}, u32[]{:S(2)}) %copy-start) | copy-done | bytes 614424
  3.3 0.0 copy-start.1
  3.3 1.0 %copy-done.1 = f32[5,5,2048]{2,1,0:T(8,128)S(1)} copy-done((f32[5,5,2048]{2,1,0:T(8,128)S(1)}, f32[5,5,2048]{2,1,0:T(8,128)}, u32[]{:S(2)}) %copy-start.1) | copy-done | bytes 204824
  4.3 0.0 copy-start.2
  4.3 0.9 %copy-done.2 = bf16[8,2,64,128]{3,2,1,0:T(8,128)(2,1)S(1)} copy-done((bf16[8,2,64,128]{3,2,1,0:T(8,128)(2,1)S(1)}, bf16[8,2,64,128]{3,2,1,0:T(8,128)(2,1)}, u32[]{:S(2)}) %copy-start.2) | copy-done | bytes 262168
  5.3 0.0 copy-start.3
  5.3 0.9 %copy-done.3 = f32[5,2,2,2048]{3,2,1,0:T(2,128)S(1)} copy-done((f32[5,2,2,2048]{3,2,1,0:T(2,128)S(1)}, f32[5,2,2,2048]{3,2,1,0:T(2,128)}, u32[]{:S(2)}) %copy-start.3) | copy-done | bytes 163864
  6.2 0.0 copy-start.4
  6.2 0.9 %copy-done.4 = f32[5,2,2,2048]{3,2,1,0:T(2,128)S(1)} copy-done((f32[5,2,2,2048]{3,2,1,0:T(2,128)S(1)}, f32[5,2,2,2048]{3,2,1,0:T(2,128)}, u32[]{:S(2)}) %copy-start.4) | copy-done | bytes 163864
  7.1 0.0 copy-start.5
  7.1 0.9 %copy-done.5 = f32[5,2,2048]{2,1,0:T(2,128)S(1)} copy-done((f32[5,2,2048]{2,1,0:T(2,128)S(1)}, f32[5,2,2048]{2,1,0:T(2,128)}, u32[]{:S(2)}) %copy-start.5) | copy-done | bytes 81944
  8.0 0.0 copy-start.7
  8.0 0.7 %copy-done.7 = s32[4096,1]{0,1:T(1,128)S(1)} copy-done((s32[4096,1]{0,1:T(1,128)S(1)}, s32[4096,1]{0,1:T(1,128)}, u32[]{:S(2)}) %copy-start.7) | copy-done | bytes 16408
  8.7 0.0 copy-start.8
  8.7 0.7 %copy-done.8 = s32[4096]{0:T(1024)S(1)} copy-done((s32[4096]{0:T(1024)S(1)}, s32[4096]{0:T(1024)}, u32[]{:S(2)}) %copy-start.8) | copy-done | bytes 16408
  9.4 34.4 %shard_map.118 = f32[5,2,2,2048]{3,2,1,0:T(2,128)S(1)} custom-call(f32[8]{0:T(128)S(1)} %copy-done.10, bf16[8,128,128]{2,1,0:T(8,128)(2,1)S(1)} %bitcast.14, bf16[32,128]{1,0:T(8,128)(2,1)S(1)} %mul.20.coeff_ref, s32[32,128]{1,0:T(8,128)S(1)} %bitcast.15, s32[32,128]{1,0:T(8,128)S(1)} %bitcast.16, f32[5,2,2048]{2,1,0:T(2,128)S(1)} %copy-done.5, ...), custom_call_target="tpu_custom_call" | custom-call | tf_op jit(solution)/shard_map/pallas_call | solution.py:513
  43.8 0.7 %copy.17 = f32[5,2,2,2048]{3,2,1,0:T(2,128)} copy(f32[5,2,2,2048]{3,2,1,0:T(2,128)S(1)} %shard_map.118) | data formatting | bytes 327680
  (1 shorter events, 0.0 us)
Async XLA Ops:
  0.0 1.6 %copy-start.6 = (s32[6,2048]{1,0:T(8,128)S(1)}, s32[6,2048]{1,0:T(8,128)}, u32[]{:S(2)}) copy-start(s32[6,2048]{1,0:T(8,128)} %neighbor_ref.1) | copy-start | bytes 147460
  1.5 0.7 %copy-start.9 = (s32[4,256]{1,0:T(4,128)S(1)}, s32[4,256]{1,0:T(4,128)}, u32[]{:S(2)}) copy-start(s32[4,256]{1,0:T(4,128)} %send_ref.1) | copy-start | bytes 12292
  1.5 0.7 %copy-start.10 = (f32[8]{0:T(128)S(1)}, f32[8]{0:T(128)}, u32[]{:S(2)}) copy-start(f32[8]{0:T(128)} %freq_ref.1) | copy-start | bytes 100
  2.2 1.1 %copy-start = (bf16[6,5,5,2048]{3,0,2,1:T(8,128)(2,1)S(1)}, bf16[6,5,5,2048]{3,0,2,1:T(8,128)(2,1)}, u32[]{:S(2)}) copy-start(bf16[6,5,5,2048]{3,0,2,1:T(8,128)(2,1)} %param.21) | copy-start | bytes 1843204
  3.3 1.0 %copy-start.1 = (f32[5,5,2048]{2,1,0:T(8,128)S(1)}, f32[5,5,2048]{2,1,0:T(8,128)}, u32[]{:S(2)}) copy-start(f32[5,5,2048]{2,1,0:T(8,128)} %diag_ref.1) | copy-start | bytes 614404
  4.3 0.9 %copy-start.2 = (bf16[8,2,64,128]{3,2,1,0:T(8,128)(2,1)S(1)}, bf16[8,2,64,128]{3,2,1,0:T(8,128)(2,1)}, u32[]{:S(2)}) copy-start(bf16[8,2,64,128]{3,2,1,0:T(8,128)(2,1)} %param.12) | copy-start | bytes 786436
  5.3 0.9 %copy-start.3 = (f32[5,2,2,2048]{3,2,1,0:T(2,128)S(1)}, f32[5,2,2,2048]{3,2,1,0:T(2,128)}, u32[]{:S(2)}) copy-start(f32[5,2,2,2048]{3,2,1,0:T(2,128)} %flow_ref.1) | copy-start | bytes 491524
  6.2 0.9 %copy-start.4 = (f32[5,2,2,2048]{3,2,1,0:T(2,128)S(1)}, f32[5,2,2,2048]{3,2,1,0:T(2,128)}, u32[]{:S(2)}) copy-start(f32[5,2,2,2048]{3,2,1,0:T(2,128)} %prev_ref.1) | copy-start | bytes 491524
  7.1 0.9 %copy-start.5 = (f32[5,2,2048]{2,1,0:T(2,128)S(1)}, f32[5,2,2048]{2,1,0:T(2,128)}, u32[]{:S(2)}) copy-start(f32[5,2,2048]{2,1,0:T(2,128)} %weight_ref.1) | copy-start | bytes 245764
  8.0 0.7 %copy-start.7 = (s32[4096,1]{0,1:T(1,128)S(1)}, s32[4096,1]{0,1:T(1,128)}, u32[]{:S(2)}) copy-start(s32[4096,1]{0,1:T(1,128)} %param.15) | copy-start | bytes 49156
  8.7 0.7 %copy-start.8 = (s32[4096]{0:T(1024)S(1)}, s32[4096]{0:T(1024)}, u32[]{:S(2)}) copy-start(s32[4096]{0:T(1024)} %param.16) | copy-start | bytes 49156

commit v3 on v2

--- a/solution.py
+++ b/solution.py
@@ -57,6 +57,11 @@
         while count * self.steps % 8:
             count += 1
         self.slot_rows = count * self.steps
+        spare = self.slot_rows - (self.values + 1) * self.steps
+        self.compact = self.width == 2 * LANES and spare == self.steps
+        self.sent_rows = self.slot_rows * (self.width // LANES)
+        if self.compact:
+            self.sent_rows -= 2 * self.steps
         self.chunks = self.cells // LANES
         self.wide = min(2 * LANES, self.halo)
         self.face_chunks = self.faces // LANES
@@ -64,52 +69,61 @@
 
 def kernel(
     pn,
-    freq_ref,
-    spline_ref,
-    coeff_ref,
-    dest_ref,
-    cell_ref,
-    weight_ref,
-    flow_ref,
-    prev_ref,
-    diag_ref,
-    jac_ref,
-    neighbor_ref,
-    send_ref,
-    out_ref,
-    part_buf,
-    face_buf,
-    slot_buf,
-    left_buf,
-    right_buf,
-    pack_buf,
-    recv_buf,
-    add_left,
-    add_right,
-    wall_buf,
-    field,
-    table,
-    table_far,
-    hot_send,
-    hot_near,
-    high_buf,
-    near,
-    ghost,
-    halo_send,
-    beside,
-    jac,
-    diag,
-    weight,
-    flow,
-    iterate,
-    coupled,
-    rep_send_sem,
-    rep_recv_sem,
-    dom_send_sem,
-    dom_recv_sem,
-    halo_send_sem,
-    halo_recv_sem,
+    *refs,
 ):
+    hbm, out_ref, staged, (load_sem, *refs) = refs[:12], refs[12], refs[13:25], refs[25:]
+    (
+        freq_ref,
+        coeff_ref,
+        spline_ref,
+        dest_ref,
+        cell_ref,
+        prev_ref,
+        send_ref,
+        neighbor_ref,
+        jac_ref,
+        diag_ref,
+        weight_ref,
+        flow_ref,
+    ) = staged
+    (
+        part_buf,
+        face_buf,
+        slot_buf,
+        left_buf,
+        right_buf,
+        slot_sum,
+        pack_buf,
+        recv_buf,
+        add_left,
+        add_right,
+        wall_buf,
+        field,
+        table,
+        table_far,
+        hot_send,
+        hot_near,
+        high_buf,
+        near,
+        ghost,
+        halo_send,
+        beside,
+        jac,
+        diag,
+        weight,
+        flow,
+        iterate,
+        coupled,
+        rep_send_sem,
+        rep_recv_sem,
+        dom_send_sem,
+        dom_recv_sem,
+        halo_send_sem,
+        halo_recv_sem,
+    ) = refs
+    loads = [pltpu.make_async_copy(hbm[i], staged[i], load_sem.at[i]) for i in range(12)]
+    for load in loads:
+        load.start()
     me_dom, me_rep = lax.axis_index("dom"), lax.axis_index("rep")
     n_ch, rows, rpad, width = pn.chunks, pn.rows, pn.row_pad, pn.part_rows
     groups = rpad // 8
@@ -131,12 +145,29 @@
     row_id = iota((pn.rep * pn.values, LANES), 0)
     pair_id = row_id // pn.values * pn.pairs + row_id % pn.pairs
     scale = jnp.zeros(row_id.shape, F32)
+    loads[0].wait()
     for pair in range(pn.rep * pn.pairs):
         scale = jnp.where(pair_id == pair, freq_ref[pair], scale)
     scale = jnp.where(row_id // pn.pairs % 2 == 0, -scale, scale)
     scale = jnp.where(row_id // width % 2 == 0, scale, 1.0)
+    loads[1].wait()
+    all_pairs = pn.rep * pn.pairs
+    shape = (pn.rep * pn.values, 2 * all_pairs)
+    row_id, column = iota(shape, 0), iota(shape, 1)
+    part_id = row_id // pn.pairs % 2
+    pair_id = row_id // pn.values * pn.pairs + row_id % pn.pairs
+    coeffs = []
+    for q in range(2):
+        source = part_id if q == 1 else 1 - part_id
+        chosen = (row_id // width % 2 == q) & (column == source * all_pairs + pair_id)
+        chosen = jnp.where(chosen, 1.0, 0.0).astype(BF16)
+        coeffs.append(jnp.dot(chosen, coeff_ref[...], preferred_element_type=F32).astype(BF16))
+    modes = coeff_ref.shape[1]
+    loads[2].wait()
     for block in range(pn.blocks):
-        base = jnp.dot(coeff_ref[...], spline_ref[block], preferred_element_type=F32) * scale
+        base = jnp.dot(coeffs[0], spline_ref[block, :modes], preferred_element_type=F32)
+        base += jnp.dot(coeffs[1], spline_ref[block, modes:], preferred_element_type=F32)
+        base *= scale
         for peer in range(pn.rep):
             part_buf[peer, :, block * LANES : (block + 1) * LANES] = base[
                 peer * pn.values : (peer + 1) * pn.values
@@ -174,7 +205,9 @@
         1.0,
         0.0,
     ).astype(BF16)
-    dest = dest_ref[...]
+    loads[3].wait()
+    ahead = pn.dom // 4
+    dest = remainder(dest_ref[...] - me_dom + (2 * pn.dom - ahead), pn.dom)
     slots = jnp.zeros((lines, LANES), F32)
     for first in range(0, pn.dom, group):
         mask = jnp.concatenate(
@@ -326,25 +359,26 @@
         for row in range(rows):
             iterate[row * n_ch : (row + 1) * n_ch, :] = line(coupled, row)
 
-    for e in range(pn.comps):
-        for r in range(2):
-            unfold(prev_ref[e, r], iterate, (e * width + r * pn.pairs) * n_ch)
-    field[...] = jnp.zeros(field.shape, F32)
-    spread_field()
-    for block in range(4):
-        index = jnp.broadcast_to(send_ref[block : block + 1, :], (8, pn.halo))
-        one_hot(remainder(index, wide), hot_send.at[block])
-    send_halo(0)
+    loads[4].wait()
+
+    def low_hot(chunk, carry):
+        low = remainder(slot_buf[pl.ds(chunk, 1), :], pn.width)
+        low = jnp.broadcast_to(low, (pn.width, LANES))
+        where = pl.ds(pl.multiple_of(chunk * LANES, LANES), LANES)
+        right_buf[:, where] = jnp.where(low == iota(low.shape, 0), 1.0, 0.0).astype(BF16)
+        return carry
+
+    lax.fori_loop(0, lines, low_hot, 0)
 
     for offset in range(1, pn.rep):
         rep_copy(offset).wait()
 
     per = 8 if lines % 8 == 0 else 1
-    n_slot = pn.dom * pn.slot_rows
-    for d in range(pn.dom):
-        pack_buf[d] = jnp.zeros((pn.slot_rows, pn.width), F32)
-
-    def pack(turn, carry):
+    half_dom = pn.dom // 2
+    n_slot = half_dom * pn.slot_rows
+    slot_half = slice(0, n_slot), slice(n_slot, 2 * n_slot)
+
+    def pack(first_place, turn, carry):
         for c in range(per):
             chunk = turn * per + c
             lanes = slice(c * LANES, (c + 1) * LANES)
@@ -353,11 +387,9 @@
             column = pl.multiple_of(chunk % pn.blocks * LANES, LANES)
             value = face_buf[owner, :, pl.ds(column, LANES)]
             cell = cell_ref[pl.ds(chunk, 1), :].astype(F32)
-            low = jnp.broadcast_to(remainder(slot, pn.width), (pn.width, LANES))
-            right_buf[:, lanes] = jnp.where(low == iota((pn.width, LANES), 0), 1.0, 0.0).astype(BF16)
             high = jnp.broadcast_to(quotient(slot, pn.width), (8, LANES))
             sub = iota((8, LANES), 0)
-            tiles = []
+            parts = []
             for tile in range(pn.slot_rows // 8):
                 row = jnp.zeros((8, LANES), F32)
                 for v in range(pn.values + 1):
@@ -367,44 +399,75 @@
                         continue
                     inside = (sub >= low_row) & (sub < top_row)
                     row = jnp.where(inside, jnp.broadcast_to(source, (8, LANES)), row)
-                tiles.append(row)
-            parts = [split(t) for t in tiles]
-            parts = [(a.astype(F32), b.astype(F32)) for a, b in parts]
+                parts.append([part.astype(F32) for part in split(row)])
             halves = ([], [])
-            for d in range(pn.dom):
+            for d in range(half_dom):
                 for tile in range(pn.slot_rows // 8):
                     step = remainder(sub + tile * 8, pn.steps)
-                    here = high == d * pn.steps + step
+                    here = high == (first_place + d) * pn.steps + step
                     for half in range(2):
                         halves[half].append(jnp.where(here, parts[tile][half], 0.0))
-            left_buf[0:n_slot, lanes] = jnp.concatenate(halves[0], axis=0).astype(BF16)
-            left_buf[n_slot : 2 * n_slot, lanes] = jnp.concatenate(halves[1], axis=0).astype(BF16)
-        found = dot_last(left_buf[...], right_buf[...])
-        for d in range(pn.dom):
-            a, b = d * pn.slot_rows, n_slot + d * pn.slot_rows
-            pack_buf[d] += found[a : a + pn.slot_rows] + found[b : b + pn.slot_rows]
+            for half in range(2):
+                left_buf[slot_half[half], lanes] = jnp.concatenate(halves[half], axis=0).astype(BF16)
+        where = pl.ds(pl.multiple_of(turn * per * LANES, per * LANES), per * LANES)
+        found = dot_last(left_buf[...], right_buf[:, where])
+        slot_sum[...] += found[:n_slot] + found[n_slot:]
         return carry
 
-    lax.fori_loop(0, lines // per, pack, 0)
-
-    def dom_copy(offset):
-        target = lax.rem(me_dom + offset, pn.dom)
+    def dom_copy(place):
+        target = lax.rem(me_dom + place + ahead, pn.dom)
         return pltpu.make_async_remote_copy(
-            src_ref=pack_buf.at[target],
-            dst_ref=recv_buf.at[offset],
-            send_sem=dom_send_sem.at[offset],
-            recv_sem=dom_recv_sem.at[offset],
+            src_ref=pack_buf.at[place],
+            dst_ref=recv_buf.at[place],
+            send_sem=dom_send_sem.at[place],
+            recv_sem=dom_recv_sem.at[place],
             device_id=(target, me_rep),
             device_id_type=MESH,
         )
 
-    def send_faces(offset, carry):
-        dom_copy(offset).start()
+    def send_faces(place, carry):
+        dom_copy(place).start()
         return carry
 
-    lax.fori_loop(1, pn.dom, send_faces, 0)
-    recv_buf[0] = pack_buf[me_dom]
-
+    own_place = pn.dom - ahead
+    filled = pn.values * pn.steps
+    for first_place in (0, half_dom):
+        slot_sum[...] = jnp.zeros(slot_sum.shape, F32)
+        lax.fori_loop(0, lines // per, functools.partial(pack, first_place), 0)
+        for d in range(half_dom):
+            a = d * pn.slot_rows
+            if pn.compact:
+                found = slot_sum[a : a + pn.slot_rows, :LANES]
+                other = slot_sum[a : a + pn.slot_rows, LANES:]
+                pack_buf[first_place + d] = jnp.concatenate(
+                    [found[: filled + pn.steps], other[filled : filled + pn.steps], other[:filled]], axis=0
+                )
+            else:
+                for part in range(pn.width // LANES):
+                    pack_buf[
+                        first_place + d, part * pn.slot_rows : (part + 1) * pn.slot_rows, :
+                    ] = slot_sum[a : a + pn.slot_rows, part * LANES : (part + 1) * LANES]
+        if first_place == 0:
+            lax.fori_loop(0, half_dom, send_faces, 0)
+        else:
+            lax.fori_loop(half_dom, own_place, send_faces, 0)
+            lax.fori_loop(own_place + 1, pn.dom, send_faces, 0)
+    recv_buf[own_place] = pack_buf[own_place]
+
+    loads[5].wait()
+    for e in range(pn.comps):
+        for r in range(2):
+            unfold(prev_ref[e, r], iterate, (e * width + r * pn.pairs) * n_ch)
+    loads[6].wait()
+    field[...] = jnp.zeros(field.shape, F32)
+    spread_field()
+    for block in range(4):
+        index = jnp.broadcast_to(send_ref[block : block + 1, :], (8, pn.halo))
+        one_hot(remainder(index, wide), hot_send.at[block])
+    send_halo(0)
+
+    for load in loads[7:]:
+        load.wait()
     def unfold_jac(index, carry):
         unfold(jac_ref[index].astype(F32), jac, index * (n_faces * n_ch))
         return carry
@@ -430,17 +493,19 @@
         for step in range(pn.steps):
             for part in range(pn.width // LANES):
                 place = step * pn.width + part * LANES
-                lanes = slice(part * LANES, (part + 1) * LANES)
-                row = pn.values * pn.steps + step
-                cell = recv_buf[offset, row : row + 1, lanes].astype(jnp.int32)
+                if pn.compact:
+                    top, cell_row = part * pn.slot_rows, filled + step + part * pn.steps
+                else:
+                    top, cell_row = part * pn.slot_rows, filled + step + part * pn.slot_rows
+                cell = recv_buf[offset, cell_row : cell_row + 1, :].astype(jnp.int32)
                 low = jnp.broadcast_to(remainder(cell, LANES), (LANES, LANES))
                 add_right[:, place : place + LANES] = jnp.where(
                     low == iota((LANES, LANES), 0), 1.0, 0.0
                 ).astype(BF16)
                 here = jnp.broadcast_to(quotient(cell, LANES), (n_ch, LANES)) == iota((n_ch, LANES), 0)
                 for v in range(pn.values):
-                    row = v * pn.steps + step
-                    value = jnp.broadcast_to(recv_buf[offset, row : row + 1, lanes], (n_ch, LANES))
+                    row = top + v * pn.steps + step
+                    value = jnp.broadcast_to(recv_buf[offset, row : row + 1, :], (n_ch, LANES))
                     first, second = split(jnp.where(here, value, 0.0))
                     add_left[v * n_ch : (v + 1) * n_ch, place : place + LANES] = first
                     add_left[
@@ -449,14 +514,15 @@
         found = dot_last(add_left[...], add_right[...])
         wall_buf[...] += found[:half_rows] + found[half_rows:]
 
-    add_faces(0)
+    add_faces(own_place)
 
     def receive(offset, carry):
         dom_copy(offset).wait()
         add_faces(offset)
         return carry
 
-    lax.fori_loop(1, pn.dom, receive, 0)
+    lax.fori_loop(0, own_place, receive, 0)
+    lax.fori_loop(own_place + 1, pn.dom, receive, 0)
 
     for e in range(pn.comps):
         first, second = line(weight, 2 * e), line(weight, 2 * e + 1)
@@ -502,10 +568,22 @@
 ):
     pn = Plan(dom, rep, spline_blocks, face_dest, flow_rhs, send_list)
     modes = modal_coeff.shape[0]
-    turned = jnp.transpose(modal_coeff.reshape(modes, 2, rep, pn.pairs), (2, 1, 3, 0))
-    both = jnp.stack([turned[:, ::-1], turned], axis=1)
-    same = jnp.eye(2, dtype=BF16)[None, :, None, None, :, None]
-    coeff = (both[:, :, :, :, None, :] * same).reshape(rep * pn.values, 2 * modes)
+    operands = (
+        frequency,
+        jnp.transpose(modal_coeff, (1, 2, 0)).reshape(2 * rep * pn.pairs, modes),
+        spline_blocks.reshape(pn.blocks, 2 * modes, LANES),
+        face_dest.reshape(pn.face_chunks, LANES),
+        face_cell.reshape(pn.face_chunks, LANES),
+        previous,
+        send_list,
+        neighbor,
+        jnp.transpose(off_jacobian, (1, 2, 0, 3)).reshape(
+            pn.comps * pn.comps, neighbor.shape[0], pn.cells
+        ),
+        diag_inverse,
+        wall_weight,
+        flow_rhs,
+    )
     n_faces = neighbor.shape[0]
     lines = pn.face_chunks
     per = 8 if lines % 8 == 0 else 1
@@ -513,16 +591,20 @@
     return pl.pallas_call(
         functools.partial(kernel, pn),
         out_shape=jax.ShapeDtypeStruct(previous.shape, F32),
-        in_specs=[pl.BlockSpec(memory_space=pltpu.SMEM)] + [vmem] * 11,
+        in_specs=[pl.BlockSpec(memory_space=pltpu.HBM)] * len(operands),
         out_specs=vmem,
-        scratch_shapes=[
+        scratch_shapes=[pltpu.SMEM(frequency.shape, F32)]
+        + [pltpu.VMEM(value.shape, value.dtype) for value in operands[1:]]
+        + [
+            pltpu.SemaphoreType.DMA((len(operands),)),
             pltpu.VMEM((rep, pn.values, pn.own_faces), F32),
             pltpu.VMEM((rep, pn.values, pn.own_faces), F32),
             pltpu.VMEM((lines, LANES), jnp.int32),
-            pltpu.VMEM((2 * dom * pn.slot_rows, per * LANES), BF16),
-            pltpu.VMEM((pn.width, per * LANES), BF16),
-            pltpu.VMEM((dom, pn.slot_rows, pn.width), F32),
-            pltpu.VMEM((dom, pn.slot_rows, pn.width), F32),
+            pltpu.VMEM((dom * pn.slot_rows, per * LANES), BF16),
+            pltpu.VMEM((pn.width, pn.faces), BF16),
+            pltpu.VMEM((dom // 2 * pn.slot_rows, pn.width), F32),
+            pltpu.VMEM((dom, pn.sent_rows, LANES), F32),
+            pltpu.VMEM((dom, pn.sent_rows, LANES), F32),
             pltpu.VMEM((2 * pn.values * pn.chunks, pn.cap), BF16),
             pltpu.VMEM((LANES, pn.cap), BF16),
             pltpu.VMEM((pn.values * pn.chunks, LANES), F32),
@@ -550,22 +632,9 @@
             pltpu.SemaphoreType.DMA((SWEEPS, 4)),
         ],
         compiler_params=pltpu.CompilerParams(
-            collective_id=0, has_side_effects=True, vmem_limit_bytes=48 * 1024 * 1024
+            collective_id=0, has_side_effects=True, vmem_limit_bytes=63 * 1024 * 1024
         ),
-    )(
-        frequency,
-        spline_blocks.reshape(pn.blocks, 2 * modes, LANES),
-        coeff,
-        face_dest.reshape(lines, LANES),
-        face_cell.reshape(lines, LANES),
-        wall_weight,
-        flow_rhs,
-        previous,
-        diag_inverse,
-        jnp.transpose(off_jacobian, (1, 2, 0, 3)).reshape(pn.comps * pn.comps, n_faces, pn.cells),
-        neighbor,
-        send_list,
-    )
+    )(*operands)
 
 
 def solution(mesh):

time: 45 us -> 38.4 us (0.85)
  local copies, waits for them, and re-layouts: 9.29 us -> 1.59 us
  Pallas kernels: 34.4 us -> 36.6 us
  other arithmetic: 0.77 us -> 0 us
    unnamed x23 -> x1, local copies, waits for them, and re-layouts: 8.48 us -> 1.59 us
    pallas_call x1, Pallas kernels: 34.4 us -> 36.6 us  [shards(): pl.pallas_call(functools.partial(kernel, pn), out_shape=jax.ShapeDtypeStr...]
    mul x1 -> x0, other arithmetic: 0.77 us -> none  [shards(): both[:, :, :, :, None, :] * same]
    another operation x1 -> x0, local copies, waits for them, and re-layouts: 0.72 us -> none  [shards(): both = jnp.stack([turned[:, ::-1], turned], axis=1)]
where the time goes in v3:
time: 38.4 us; the launch traced here: 38.2 us
  Pallas kernels  36.6 us (95%)
  local copies, waits for them, and re-layouts  1.59 us (4%)
    pallas_call x1, Pallas kernels, shards(): pl.pallas_call(functools.partial(kernel, pn), out_shape=jax.ShapeDtypeStr...  36.6 us
    unnamed x1, local copies, waits for them, and re-layouts  1.59 us

profile of v3, /device:TPU:0, one launch (start us, length us, event | category | flops | bytes accessed | tf_op | source)
XLA Modules:
  0.0 38.2 jit_solution(7734508408107168029)
XLA Ops:
  0.0 36.6 %shard_map.118 = f32[5,2,2,2048]{3,2,1,0:T(2,128)} custom-call(f32[8]{0:T(128)} %refs_0_.1, bf16[16,64]{1,0:T(8,128)(2,1)} %bitcast.13, bf16[8,128,128]{2,1,0:T(8,128)(2,1)} %bitcast.10, s32[32,128]{1,0:T(8,128)} %bitcast.11, s32[32,128]{1,0:T(8,128)} %bitcast.12, f32[5,2,2,2048]{3,2,1,0:T(2,128)} %refs_5_.1, s32[4,256]{1,0:T(4,128)} %refs_6_.1, ...), custom_call_target="tpu_custom_call" | custom-call | tf_op jit(solution)/shard_map/pallas_call | solution.py:591
  36.6 1.6 %copy.14 = f32[5,2,2,2048]{3,2,1,0:T(2,128)} copy(f32[5,2,2,2048]{3,2,1,0:T(2,128)} %shard_map.118) | data formatting | bytes 327680

commit v4 on v3

--- a/solution.py
+++ b/solution.py
@@ -100,7 +100,6 @@
         wall_buf,
         field,
         table,
-        table_far,
         hot_send,
         hot_near,
         high_buf,
@@ -231,9 +230,15 @@
     per_wide = wide // LANES
     n_faces = neighbor_ref.shape[0]
 
+    n_full = rows // 8
+    sub = iota((8, wide), 0)
+
     def spread_field():
         for row in range(rows):
-            field[pl.ds(row, n_ch, stride=rpad), :] = iterate[row * n_ch : (row + 1) * n_ch]
+            value = iterate[row * n_ch : (row + 1) * n_ch]
+            field[pl.ds(row, n_ch, stride=rpad), :] = value
+            if row >= n_full * 8:
+                field[pl.ds(row + 4, n_ch, stride=rpad), :] = value
         blocks = [
             jnp.concatenate(
                 [
@@ -244,29 +249,59 @@
             )
             for c in range(n_wide)
         ]
-        table[:, :wide], table[:, wide:] = split(jnp.concatenate(blocks, axis=0))
-
-    def pick(parts, first_chunk, count, hot, high, start):
-        found = jnp.dot(parts, jnp.concatenate([hot, hot], axis=0), preferred_element_type=F32)
+        fill_table(blocks, 0)
+
+    def fill_table(blocks, first):
+        count = len(blocks)
+        tiles = [block[g * 8 : g * 8 + 8] for g in range(n_full) for block in blocks]
+        for c in range(count // 2):
+            a, b = blocks[c][n_full * 8 :], blocks[c + count // 2][n_full * 8 :]
+            tiles.append(jnp.where(sub < 4, a, b))
+        where = slice(first, first + len(tiles) * 8)
+        table[where, :wide], table[where, wide:] = split(jnp.concatenate(tiles, axis=0))
+
+    def table_rows(count):
+        return (n_full * count + count // 2) * 8
+
+    near_rows, far_rows = table_rows(n_wide), table_rows(4 * pn.halo // wide)
+
+    def multiply(first, count, hot):
+        return jnp.dot(
+            table[first : first + count, :],
+            jnp.concatenate([hot, hot], axis=0),
+            preferred_element_type=F32,
+        )
+
+    def choose(found, first_chunk, count, high, start):
         picked = list(start)
+        late = jnp.where(iota(high.shape, 0) < 4, high, high - count // 2)
         for chunk in range(count):
             here = high == first_chunk + chunk
-            for g in range(groups):
-                at = chunk * rpad + g * 8
+            for g in range(n_full):
+                at = (g * count + chunk) * 8
                 picked[g] = jnp.where(here, found[at : at + 8], picked[g])
+        for chunk in range(count // 2):
+            at = (n_full * count + chunk) * 8
+            picked[n_full] = jnp.where(
+                late == first_chunk + chunk, found[at : at + 8], picked[n_full]
+            )
         return picked
+
+    def joined(picked):
+        return picked[:n_full] + [picked[n_full] + pltpu.roll(picked[n_full], 4, axis=0)]
 
     def one_hot(low, target):
         both = jnp.concatenate([low, low], axis=0)
 
         def body(turn, carry):
-            first = pl.multiple_of(turn * 16, 16)
-            target[pl.ds(first, 16), :] = jnp.where(
-                both == iota(both.shape, 0) + first, 1.0, 0.0
-            ).astype(BF16)
+            for part in range(4):
+                first = pl.multiple_of(turn * 64 + part * 16, 16)
+                target[pl.ds(first, 16), :] = jnp.where(
+                    both == iota(both.shape, 0) + first, 1.0, 0.0
+                ).astype(BF16)
             return carry
 
-        lax.fori_loop(0, wide // 16, body, 0)
+        lax.fori_loop(0, wide // 64, body, 0)
 
     def halo_copy(sweep, block):
         return pltpu.make_async_remote_copy(
@@ -278,45 +313,68 @@
             device_id_type=MESH,
         )
 
+    def send_index():
+        return jnp.concatenate(
+            [jnp.broadcast_to(send_ref[k : k + 1, :], (8, pn.halo)) for k in range(4)], axis=1
+        )
+
     def send_halo(sweep):
+        high = quotient(send_index(), wide)
+        zeros = [jnp.zeros(high.shape, F32)] * groups
+        found = joined(choose(multiply(0, near_rows, hot_send[...]), 0, n_wide, high, zeros))
         for block in range(4):
-            index = jnp.broadcast_to(send_ref[block : block + 1, :], (8, pn.halo))
-            zeros = [jnp.zeros((8, pn.halo), F32)] * groups
-            found = pick(table[...], 0, n_wide, hot_send[block], quotient(index, wide), zeros)
             for g in range(groups):
-                halo_send[sweep, block, g * 8 : g * 8 + 8, :] = found[g]
+                halo_send[sweep, block, g * 8 : g * 8 + 8, :] = found[g][
+                    :, block * pn.halo : (block + 1) * pn.halo
+                ]
             halo_copy(sweep, block).start()
 
-    def gather_local():
-        def body(face, carry):
-            high = high_buf[face]
-            zeros = [jnp.zeros(high.shape, F32)] * groups
-            found = pick(table[...], 0, n_wide, hot_near[face], high, zeros)
-            for g in range(groups):
-                near[face, g * 8 : g * 8 + 8, :] = found[g]
-            return carry
-
-        lax.fori_loop(0, n_faces, body, 0)
-
     n_ghost = pn.halo // wide
 
-    def gather_ghost(sweep):
+    def take_ghost(sweep):
         for block in range(4):
             halo_copy(sweep, block).wait()
         blocks = []
         for chunk in range(4 * n_ghost):
             lane = chunk % n_ghost * wide
             blocks.append(ghost[sweep, chunk // n_ghost, :, lane : lane + wide])
-        table_far[:, :wide], table_far[:, wide:] = split(jnp.concatenate(blocks, axis=0))
-
+        fill_table(blocks, near_rows)
+
+    def keep_beside(face, picked):
+        found = joined(picked)
+        for g in range(groups):
+            count = min(8, rows - g * 8)
+            for tile in range(n_ch):
+                where = pl.ds((face * rows + g * 8) * n_ch + tile, count, stride=n_ch)
+                beside[where, :] = found[g][:count, tile * LANES : (tile + 1) * LANES]
+
+    def gather_local():
+        def body(face, carry):
+            high = high_buf[face]
+            zeros = [jnp.zeros(high.shape, F32)] * groups
+            found = choose(multiply(0, near_rows, hot_near[face]), 0, n_wide, high, zeros)
+            for g in range(groups):
+                near[face, g * 8 : g * 8 + 8, :] = found[g]
+            return carry
+
+        lax.fori_loop(0, n_faces, body, 0)
+
+    def gather_ghost():
         def body(face, carry):
             start = [near[face, g * 8 : g * 8 + 8, :] for g in range(groups)]
-            found = pick(table_far[...], n_wide, 4 * n_ghost, hot_near[face], high_buf[face], start)
-            for g in range(groups):
-                count = min(8, rows - g * 8)
-                for tile in range(n_ch):
-                    where = pl.ds((face * rows + g * 8) * n_ch + tile, count, stride=n_ch)
-                    beside[where, :] = found[g][:count, tile * LANES : (tile + 1) * LANES]
+            found = multiply(near_rows, far_rows, hot_near[face])
+            keep_beside(face, choose(found, n_wide, 4 * n_ghost, high_buf[face], start))
+            return carry
+
+        lax.fori_loop(0, n_faces, body, 0)
+
+    def gather_all():
+        def body(face, carry):
+            high = high_buf[face]
+            zeros = [jnp.zeros(high.shape, F32)] * groups
+            found = multiply(0, near_rows + far_rows, hot_near[face])
+            some = choose(found[:near_rows], 0, n_wide, high, zeros)
+            keep_beside(face, choose(found[near_rows:], n_wide, 4 * n_ghost, high, some))
             return carry
 
         lax.fori_loop(0, n_faces, body, 0)
@@ -361,19 +419,22 @@
 
     loads[4].wait()
 
-    def low_hot(chunk, carry):
-        low = remainder(slot_buf[pl.ds(chunk, 1), :], pn.width)
-        low = jnp.broadcast_to(low, (pn.width, LANES))
-        where = pl.ds(pl.multiple_of(chunk * LANES, LANES), LANES)
-        right_buf[:, where] = jnp.where(low == iota(low.shape, 0), 1.0, 0.0).astype(BF16)
+    per = 4 if lines % 4 == 0 else 1
+
+    def low_hot(turn, carry):
+        for c in range(per):
+            chunk = turn * per + c
+            low = remainder(slot_buf[pl.ds(chunk, 1), :], pn.width)
+            low = jnp.broadcast_to(low, (pn.width, LANES))
+            where = pl.ds(pl.multiple_of(chunk * LANES, LANES), LANES)
+            right_buf[:, where] = jnp.where(low == iota(low.shape, 0), 1.0, 0.0).astype(BF16)
         return carry
 
-    lax.fori_loop(0, lines, low_hot, 0)
+    lax.fori_loop(0, lines // per, low_hot, 0)
 
     for offset in range(1, pn.rep):
         rep_copy(offset).wait()
 
-    per = 8 if lines % 8 == 0 else 1
     half_dom = pn.dom // 2
     n_slot = half_dom * pn.slot_rows
     slot_half = slice(0, n_slot), slice(n_slot, 2 * n_slot)
@@ -381,7 +442,7 @@
     def pack(first_place, turn, carry):
         for c in range(per):
             chunk = turn * per + c
-            lanes = slice(c * LANES, (c + 1) * LANES)
+            lanes = pl.ds(pl.multiple_of(chunk * LANES, LANES), LANES)
             slot = slot_buf[pl.ds(chunk, 1), :]
             owner = chunk // pn.blocks
             column = pl.multiple_of(chunk % pn.blocks * LANES, LANES)
@@ -409,9 +470,6 @@
                         halves[half].append(jnp.where(here, parts[tile][half], 0.0))
             for half in range(2):
                 left_buf[slot_half[half], lanes] = jnp.concatenate(halves[half], axis=0).astype(BF16)
-        where = pl.ds(pl.multiple_of(turn * per * LANES, per * LANES), per * LANES)
-        found = dot_last(left_buf[...], right_buf[:, where])
-        slot_sum[...] += found[:n_slot] + found[n_slot:]
         return carry
 
     def dom_copy(place):
@@ -432,8 +490,9 @@
     own_place = pn.dom - ahead
     filled = pn.values * pn.steps
     for first_place in (0, half_dom):
-        slot_sum[...] = jnp.zeros(slot_sum.shape, F32)
         lax.fori_loop(0, lines // per, functools.partial(pack, first_place), 0)
+        found = dot_last(left_buf[...], right_buf[...])
+        slot_sum[...] = found[:n_slot] + found[n_slot:]
         for d in range(half_dom):
             a = d * pn.slot_rows
             if pn.compact:
@@ -461,9 +520,7 @@
     loads[6].wait()
     field[...] = jnp.zeros(field.shape, F32)
     spread_field()
-    for block in range(4):
-        index = jnp.broadcast_to(send_ref[block : block + 1, :], (8, pn.halo))
-        one_hot(remainder(index, wide), hot_send.at[block])
+    one_hot(remainder(send_index(), wide), hot_send)
     send_halo(0)
 
     for load in loads[7:]:
@@ -482,24 +539,24 @@
         unfold(weight_ref[e], weight, e * 2 * n_ch)
         for r in range(2):
             unfold(flow_ref[e, r], flow, (e * width + r * pn.pairs) * n_ch)
-    gather_local()
-    gather_ghost(0)
+    take_ghost(0)
+    gather_all()
     couple()
 
-    wall_buf[...] = jnp.zeros(wall_buf.shape, F32)
     half_rows = pn.values * n_ch
 
     def add_faces(offset):
         for step in range(pn.steps):
             for part in range(pn.width // LANES):
-                place = step * pn.width + part * LANES
+                place = offset * pn.cap + step * pn.width + part * LANES
+                where = pl.ds(pl.multiple_of(place, LANES), LANES)
                 if pn.compact:
                     top, cell_row = part * pn.slot_rows, filled + step + part * pn.steps
                 else:
                     top, cell_row = part * pn.slot_rows, filled + step + part * pn.slot_rows
                 cell = recv_buf[offset, cell_row : cell_row + 1, :].astype(jnp.int32)
                 low = jnp.broadcast_to(remainder(cell, LANES), (LANES, LANES))
-                add_right[:, place : place + LANES] = jnp.where(
+                add_right[:, where] = jnp.where(
                     low == iota((LANES, LANES), 0), 1.0, 0.0
                 ).astype(BF16)
                 here = jnp.broadcast_to(quotient(cell, LANES), (n_ch, LANES)) == iota((n_ch, LANES), 0)
@@ -507,12 +564,8 @@
                     row = top + v * pn.steps + step
                     value = jnp.broadcast_to(recv_buf[offset, row : row + 1, :], (n_ch, LANES))
                     first, second = split(jnp.where(here, value, 0.0))
-                    add_left[v * n_ch : (v + 1) * n_ch, place : place + LANES] = first
-                    add_left[
-                        half_rows + v * n_ch : half_rows + (v + 1) * n_ch, place : place + LANES
-                    ] = second
-        found = dot_last(add_left[...], add_right[...])
-        wall_buf[...] += found[:half_rows] + found[half_rows:]
+                    add_left[v * n_ch : (v + 1) * n_ch, where] = first
+                    add_left[half_rows + v * n_ch : half_rows + (v + 1) * n_ch, where] = second
 
     add_faces(own_place)
 
@@ -523,6 +576,8 @@
 
     lax.fori_loop(0, own_place, receive, 0)
     lax.fori_loop(own_place + 1, pn.dom, receive, 0)
+    found = dot_last(add_left[...], add_right[...])
+    wall_buf[...] = found[:half_rows] + found[half_rows:]
 
     for e in range(pn.comps):
         first, second = line(weight, 2 * e), line(weight, 2 * e + 1)
@@ -537,7 +592,8 @@
         spread_field()
         send_halo(sweep)
         gather_local()
-        gather_ghost(sweep)
+        take_ghost(sweep)
+        gather_ghost()
         couple()
         update()
 
@@ -586,7 +642,6 @@
     )
     n_faces = neighbor.shape[0]
     lines = pn.face_chunks
-    per = 8 if lines % 8 == 0 else 1
     vmem = pl.BlockSpec(memory_space=pltpu.VMEM)
     return pl.pallas_call(
         functools.partial(kernel, pn),
@@ -600,18 +655,17 @@
             pltpu.VMEM((rep, pn.values, pn.own_faces), F32),
             pltpu.VMEM((rep, pn.values, pn.own_faces), F32),
             pltpu.VMEM((lines, LANES), jnp.int32),
-            pltpu.VMEM((dom * pn.slot_rows, per * LANES), BF16),
+            pltpu.VMEM((dom * pn.slot_rows, pn.faces), BF16),
             pltpu.VMEM((pn.width, pn.faces), BF16),
             pltpu.VMEM((dom // 2 * pn.slot_rows, pn.width), F32),
             pltpu.VMEM((dom, pn.sent_rows, LANES), F32),
             pltpu.VMEM((dom, pn.sent_rows, LANES), F32),
-            pltpu.VMEM((2 * pn.values * pn.chunks, pn.cap), BF16),
-            pltpu.VMEM((LANES, pn.cap), BF16),
+            pltpu.VMEM((2 * pn.values * pn.chunks, dom * pn.cap), BF16),
+            pltpu.VMEM((LANES, dom * pn.cap), BF16),
             pltpu.VMEM((pn.values * pn.chunks, LANES), F32),
             pltpu.VMEM((pn.chunks * pn.row_pad, LANES), F32),
-            pltpu.VMEM((pn.cells // pn.wide * pn.row_pad, 2 * pn.wide), BF16),
-            pltpu.VMEM((4 * pn.halo // pn.wide * pn.row_pad, 2 * pn.wide), BF16),
-            pltpu.VMEM((4, pn.wide, pn.halo), BF16),
+            pltpu.VMEM(((pn.cells + 4 * pn.halo) // pn.wide * pn.rows, 2 * pn.wide), BF16),
+            pltpu.VMEM((pn.wide, 4 * pn.halo), BF16),
             pltpu.VMEM((n_faces, pn.wide, pn.cells), BF16),
             pltpu.VMEM((n_faces, 8, pn.cells), jnp.int32),
             pltpu.VMEM((n_faces, pn.row_pad, pn.cells), F32),

time: 38.4 us -> 40.2 us (1.047)
  Pallas kernels: 36.6 us -> 38.4 us
    pallas_call x1, Pallas kernels: 36.6 us -> 38.4 us  [shards(): pl.pallas_call(functools.partial(kernel, pn), out_shape=jax.ShapeDtypeStr...]
where the time goes in v4:
time: 40.2 us; the launch traced here: 40 us
  Pallas kernels  38.4 us (96%)
  local copies, waits for them, and re-layouts  1.59 us (4%)
    pallas_call x1, Pallas kernels, shards(): pl.pallas_call(functools.partial(kernel, pn), out_shape=jax.ShapeDtypeStr...  38.4 us
    unnamed x1, local copies, waits for them, and re-layouts  1.59 us

profile of v4, /device:TPU:0, one launch (start us, length us, event | category | flops | bytes accessed | tf_op | source)
XLA Modules:
  0.0 40.0 jit_solution(16181001734885009432)
XLA Ops:
  0.0 38.4 %shard_map.118 = f32[5,2,2,2048]{3,2,1,0:T(2,128)} custom-call(f32[8]{0:T(128)} %refs_0_.1, bf16[16,64]{1,0:T(8,128)(2,1)} %bitcast.13, bf16[8,128,128]{2,1,0:T(8,128)(2,1)} %bitcast.10, s32[32,128]{1,0:T(8,128)} %bitcast.11, s32[32,128]{1,0:T(8,128)} %bitcast.12, f32[5,2,2,2048]{3,2,1,0:T(2,128)} %refs_5_.1, s32[4,256]{1,0:T(4,128)} %refs_6_.1, ...), custom_call_target="tpu_custom_call" | custom-call | tf_op jit(solution)/shard_map/pallas_call | solution.py:646
  38.4 1.6 %copy.14 = f32[5,2,2,2048]{3,2,1,0:T(2,128)} copy(f32[5,2,2,2048]{3,2,1,0:T(2,128)} %shard_map.118) | data formatting | bytes 327680

commit v5 on v4

--- a/solution.py
+++ b/solution.py
@@ -435,6 +435,7 @@
     for offset in range(1, pn.rep):
         rep_copy(offset).wait()
 
+    per = 8 if lines % 8 == 0 else 1
     half_dom = pn.dom // 2
     n_slot = half_dom * pn.slot_rows
     slot_half = slice(0, n_slot), slice(n_slot, 2 * n_slot)
@@ -442,7 +443,7 @@
     def pack(first_place, turn, carry):
         for c in range(per):
             chunk = turn * per + c
-            lanes = pl.ds(pl.multiple_of(chunk * LANES, LANES), LANES)
+            lanes = slice(c * LANES, (c + 1) * LANES)
             slot = slot_buf[pl.ds(chunk, 1), :]
             owner = chunk // pn.blocks
             column = pl.multiple_of(chunk % pn.blocks * LANES, LANES)
@@ -470,6 +471,9 @@
                         halves[half].append(jnp.where(here, parts[tile][half], 0.0))
             for half in range(2):
                 left_buf[slot_half[half], lanes] = jnp.concatenate(halves[half], axis=0).astype(BF16)
+        where = pl.ds(pl.multiple_of(turn * per * LANES, per * LANES), per * LANES)
+        found = dot_last(left_buf[...], right_buf[:, where])
+        slot_sum[...] += found[:n_slot] + found[n_slot:]
         return carry
 
     def dom_copy(place):
@@ -490,9 +494,8 @@
     own_place = pn.dom - ahead
     filled = pn.values * pn.steps
     for first_place in (0, half_dom):
+        slot_sum[...] = jnp.zeros(slot_sum.shape, F32)
         lax.fori_loop(0, lines // per, functools.partial(pack, first_place), 0)
-        found = dot_last(left_buf[...], right_buf[...])
-        slot_sum[...] = found[:n_slot] + found[n_slot:]
         for d in range(half_dom):
             a = d * pn.slot_rows
             if pn.compact:
@@ -514,9 +517,13 @@
     recv_buf[own_place] = pack_buf[own_place]
 
     loads[5].wait()
-    for e in range(pn.comps):
+
+    def unfold_previous(e, carry):
         for r in range(2):
             unfold(prev_ref[e, r], iterate, (e * width + r * pn.pairs) * n_ch)
+        return carry
+
+    lax.fori_loop(0, pn.comps, unfold_previous, 0)
     loads[6].wait()
     field[...] = jnp.zeros(field.shape, F32)
     spread_field()
@@ -534,22 +541,27 @@
         index = jnp.broadcast_to(neighbor_ref[face : face + 1, :], (8, pn.cells))
         high_buf[face] = quotient(index, wide)
         one_hot(remainder(index, wide), hot_near.at[face])
-    for e in range(pn.comps):
+
+    def unfold_others(e, carry):
         unfold(diag_ref[e], diag, e * pn.comps * n_ch)
         unfold(weight_ref[e], weight, e * 2 * n_ch)
         for r in range(2):
             unfold(flow_ref[e, r], flow, (e * width + r * pn.pairs) * n_ch)
+        return carry
+
+    lax.fori_loop(0, pn.comps, unfold_others, 0)
     take_ghost(0)
     gather_all()
     couple()
 
+    wall_buf[...] = jnp.zeros(wall_buf.shape, F32)
     half_rows = pn.values * n_ch
 
     def add_faces(offset):
         for step in range(pn.steps):
             for part in range(pn.width // LANES):
-                place = offset * pn.cap + step * pn.width + part * LANES
-                where = pl.ds(pl.multiple_of(place, LANES), LANES)
+                place = step * pn.width + part * LANES
+                where = slice(place, place + LANES)
                 if pn.compact:
                     top, cell_row = part * pn.slot_rows, filled + step + part * pn.steps
                 else:
@@ -566,26 +578,29 @@
                     first, second = split(jnp.where(here, value, 0.0))
                     add_left[v * n_ch : (v + 1) * n_ch, where] = first
                     add_left[half_rows + v * n_ch : half_rows + (v + 1) * n_ch, where] = second
-
-    add_faces(own_place)
+        found = dot_last(add_left[...], add_right[...])
+        wall_buf[...] += found[:half_rows] + found[half_rows:]
 
     def receive(offset, carry):
-        dom_copy(offset).wait()
+        @pl.when(offset != own_place)
+        def arrived():
+            dom_copy(offset).wait()
+
         add_faces(offset)
         return carry
 
-    lax.fori_loop(0, own_place, receive, 0)
-    lax.fori_loop(own_place + 1, pn.dom, receive, 0)
-    found = dot_last(add_left[...], add_right[...])
-    wall_buf[...] = found[:half_rows] + found[half_rows:]
-
-    for e in range(pn.comps):
+    lax.fori_loop(0, pn.dom, receive, 0)
+
+    def add_wall(e, carry):
         first, second = line(weight, 2 * e), line(weight, 2 * e + 1)
         for k in range(width):
             row = e * width + k
-            flow[row * n_ch : (row + 1) * n_ch, :] = (
+            flow[pl.ds(pl.multiple_of(row * n_ch, n_ch), n_ch), :] = (
                 line(flow, row) + first * line(wall_buf, k) + second * line(wall_buf, width + k)
             )
+        return carry
+
+    lax.fori_loop(0, pn.comps, add_wall, 0)
 
     update()
     for sweep in range(1, SWEEPS):
@@ -597,13 +612,16 @@
         couple()
         update()
 
-    for e in range(pn.comps):
+    def fold_output(e, carry):
         for r in range(2):
             for tile in range(n_ch):
                 start = (e * width + r * pn.pairs) * n_ch + tile
                 out_ref[e, r, :, tile * LANES : (tile + 1) * LANES] = iterate[
                     pl.ds(start, pn.pairs, stride=n_ch), :
                 ]
+        return carry
+
+    lax.fori_loop(0, pn.comps, fold_output, 0)
 
 
 def shards(
@@ -642,6 +660,7 @@
     )
     n_faces = neighbor.shape[0]
     lines = pn.face_chunks
+    per = 8 if pn.face_chunks % 8 == 0 else 1
     vmem = pl.BlockSpec(memory_space=pltpu.VMEM)
     return pl.pallas_call(
         functools.partial(kernel, pn),
@@ -655,13 +674,13 @@
             pltpu.VMEM((rep, pn.values, pn.own_faces), F32),
             pltpu.VMEM((rep, pn.values, pn.own_faces), F32),
             pltpu.VMEM((lines, LANES), jnp.int32),
-            pltpu.VMEM((dom * pn.slot_rows, pn.faces), BF16),
+            pltpu.VMEM((dom * pn.slot_rows, per * LANES), BF16),
             pltpu.VMEM((pn.width, pn.faces), BF16),
             pltpu.VMEM((dom // 2 * pn.slot_rows, pn.width), F32),
             pltpu.VMEM((dom, pn.sent_rows, LANES), F32),
             pltpu.VMEM((dom, pn.sent_rows, LANES), F32),
-            pltpu.VMEM((2 * pn.values * pn.chunks, dom * pn.cap), BF16),
-            pltpu.VMEM((LANES, dom * pn.cap), BF16),
+            pltpu.VMEM((2 * pn.values * pn.chunks, pn.cap), BF16),
+            pltpu.VMEM((LANES, pn.cap), BF16),
             pltpu.VMEM((pn.values * pn.chunks, LANES), F32),
             pltpu.VMEM((pn.chunks * pn.row_pad, LANES), F32),
             pltpu.VMEM(((pn.cells + 4 * pn.halo) // pn.wide * pn.rows, 2 * pn.wide), BF16),

time: 40.2 us -> 39.5 us (0.983)
  Pallas kernels: 38.4 us -> 37.7 us
    pallas_call x1, Pallas kernels: 38.4 us -> 37.7 us  [shards(): pl.pallas_call(functools.partial(kernel, pn), out_shape=jax.ShapeDtypeStr...]
where the time goes in v5:
time: 39.5 us; the launch traced here: 39.3 us
  Pallas kernels  37.7 us (95%)
  local copies, waits for them, and re-layouts  1.59 us (4%)
    pallas_call x1, Pallas kernels, shards(): pl.pallas_call(functools.partial(kernel, pn), out_shape=jax.ShapeDtypeStr...  37.7 us
    unnamed x1, local copies, waits for them, and re-layouts  1.59 us

profile of v5, /device:TPU:0, one launch (start us, length us, event | category | flops | bytes accessed | tf_op | source)
XLA Modules:
  0.0 39.3 jit_solution(16182856590016288496)
XLA Ops:
  0.0 37.7 %shard_map.118 = f32[5,2,2,2048]{3,2,1,0:T(2,128)} custom-call(f32[8]{0:T(128)} %refs_0_.1, bf16[16,64]{1,0:T(8,128)(2,1)} %bitcast.13, bf16[8,128,128]{2,1,0:T(8,128)(2,1)} %bitcast.10, s32[32,128]{1,0:T(8,128)} %bitcast.11, s32[32,128]{1,0:T(8,128)} %bitcast.12, f32[5,2,2,2048]{3,2,1,0:T(2,128)} %refs_5_.1, s32[4,256]{1,0:T(4,128)} %refs_6_.1, ...), custom_call_target="tpu_custom_call" | custom-call | tf_op jit(solution)/shard_map/pallas_call | solution.py:665
  37.7 1.6 %copy.14 = f32[5,2,2,2048]{3,2,1,0:T(2,128)} copy(f32[5,2,2,2048]{3,2,1,0:T(2,128)} %shard_map.118) | data formatting | bytes 327680

commit v6 on v5

--- a/solution.py
+++ b/solution.py
@@ -368,17 +368,6 @@
 
         lax.fori_loop(0, n_faces, body, 0)
 
-    def gather_all():
-        def body(face, carry):
-            high = high_buf[face]
-            zeros = [jnp.zeros(high.shape, F32)] * groups
-            found = multiply(0, near_rows + far_rows, hot_near[face])
-            some = choose(found[:near_rows], 0, n_wide, high, zeros)
-            keep_beside(face, choose(found[near_rows:], n_wide, 4 * n_ghost, high, some))
-            return carry
-
-        lax.fori_loop(0, n_faces, body, 0)
-
     def line(ref, index):
         return ref[pl.ds(pl.multiple_of(index * n_ch, n_ch), n_ch), :]
 
@@ -491,6 +480,21 @@
         dom_copy(place).start()
         return carry
 
+    def start_sweeps():
+        loads[5].wait()
+
+        def unfold_previous(e, carry):
+            for r in range(2):
+                unfold(prev_ref[e, r], iterate, (e * width + r * pn.pairs) * n_ch)
+            return carry
+
+        lax.fori_loop(0, pn.comps, unfold_previous, 0)
+        loads[6].wait()
+        field[...] = jnp.zeros(field.shape, F32)
+        spread_field()
+        one_hot(remainder(send_index(), wide), hot_send)
+        send_halo(0)
+
     own_place = pn.dom - ahead
     filled = pn.values * pn.steps
     for first_place in (0, half_dom):
@@ -511,24 +515,11 @@
                     ] = slot_sum[a : a + pn.slot_rows, part * LANES : (part + 1) * LANES]
         if first_place == 0:
             lax.fori_loop(0, half_dom, send_faces, 0)
+            start_sweeps()
         else:
             lax.fori_loop(half_dom, own_place, send_faces, 0)
             lax.fori_loop(own_place + 1, pn.dom, send_faces, 0)
     recv_buf[own_place] = pack_buf[own_place]
-
-    loads[5].wait()
-
-    def unfold_previous(e, carry):
-        for r in range(2):
-            unfold(prev_ref[e, r], iterate, (e * width + r * pn.pairs) * n_ch)
-        return carry
-
-    lax.fori_loop(0, pn.comps, unfold_previous, 0)
-    loads[6].wait()
-    field[...] = jnp.zeros(field.shape, F32)
-    spread_field()
-    one_hot(remainder(send_index(), wide), hot_send)
-    send_halo(0)
 
     for load in loads[7:]:
         load.wait()
@@ -550,8 +541,9 @@
         return carry
 
     lax.fori_loop(0, pn.comps, unfold_others, 0)
+    gather_local()
     take_ghost(0)
-    gather_all()
+    gather_ghost()
     couple()
 
     wall_buf[...] = jnp.zeros(wall_buf.shape, F32)

time: 39.5 us -> 37.1 us (0.939)
  Pallas kernels: 37.7 us -> 35.4 us
    pallas_call x1, Pallas kernels: 37.7 us -> 35.4 us  [shards(): pl.pallas_call(functools.partial(kernel, pn), out_shape=jax.ShapeDtypeStr...]
where the time goes in v6:
time: 37.1 us; the launch traced here: 37 us
  Pallas kernels  35.4 us (95%)
  local copies, waits for them, and re-layouts  1.59 us (4%)
    pallas_call x1, Pallas kernels, shards(): pl.pallas_call(functools.partial(kernel, pn), out_shape=jax.ShapeDtypeStr...  35.4 us
    unnamed x1, local copies, waits for them, and re-layouts  1.59 us

profile of v6, /device:TPU:0, one launch (start us, length us, event | category | flops | bytes accessed | tf_op | source)
XLA Modules:
  0.0 37.0 jit_solution(14785779178355647821)
XLA Ops:
  0.0 35.4 %shard_map.118 = f32[5,2,2,2048]{3,2,1,0:T(2,128)} custom-call(f32[8]{0:T(128)} %refs_0_.1, bf16[16,64]{1,0:T(8,128)(2,1)} %bitcast.13, bf16[8,128,128]{2,1,0:T(8,128)(2,1)} %bitcast.10, s32[32,128]{1,0:T(8,128)} %bitcast.11, s32[32,128]{1,0:T(8,128)} %bitcast.12, f32[5,2,2,2048]{3,2,1,0:T(2,128)} %refs_5_.1, s32[4,256]{1,0:T(4,128)} %refs_6_.1, ...), custom_call_target="tpu_custom_call" | custom-call | tf_op jit(solution)/shard_map/pallas_call | solution.py:657
  35.4 1.6 %copy.14 = f32[5,2,2,2048]{3,2,1,0:T(2,128)} copy(f32[5,2,2,2048]{3,2,1,0:T(2,128)} %shard_map.118) | data formatting | bytes 327680
